TPU v7x, 32 devices: a whole 2x2x4 slice. The times are simulated.
32 devices in a mesh: row: 8 (over z, core), col: 4 (over y, x).
Axes of the slice: x: 2, y: 2, z: 4, core: 2. Of those that a mesh axis runs over, the one named last changes fastest.
Arguments:
- object_slices: float32 [2, 2, 2048, 1024], P(None, None, 'row', 'col'), may hold values from -5 to 5
- probe_wave: float32 [2, 256, 256], replicated, may hold values from -6 to 6
- propagator: float32 [2, 256, 256], replicated, may hold values from -5 to 5
- measured: float32 [8, 4, 4, 256, 256], P('row', 'col'), as said below
- positions: int32 [8, 4, 4, 2], P('row', 'col'), may hold values from -128 to 128, as said below
- scan_counts: int32 [8, 4], P('row', 'col'), may hold values from 1 to 4, as said below
Outputs:
- object_grad: float32 [2, 2, 2048, 1024], P(None, None, 'row', 'col')
- probe_grad: float32 [2, 256, 256], replicated
Inputs may be any that keep to these rules, and one draw needn't show every extreme that they name: `positions`: every patch of 256 x 256 cells lies inside the object window. Slots k < scan_counts[r, c] of tile (r, c) are used, the others are ignored. `measured`: positive intensities.
All inputs are finite; a program needn't handle non-finite values.
Results may differ from a plain program's by a relative error of at most 0.0003.
Values sent between devices are 32-bit elements; how exact they have to be, the bound alone decides.
No kernel may reach another device: no remote copies, remote signals or barrier semaphores. Data moves between devices by JAX's collectives and lax.ppermute only.
A program may use at most 128 MiB of HBM per device.

v0:
```python
import math

import jax
import jax.numpy as jnp
from jax import lax
from jax.sharding import PartitionSpec as P

precision_mode = lax.Precision.HIGHEST


def padded(cells, sides, width):
    for axis, dim in sides:
        count = lax.axis_size(axis)
        ends = count - 1
        head = lax.slice_in_dim(cells, 0, width, axis=dim)
        tail = lax.slice_in_dim(cells, cells.shape[dim] - width, cells.shape[dim], axis=dim)
        cells = jnp.concatenate(
            [
                lax.ppermute(tail, axis, [(i, (i + 1) % count) for i in range(ends)]),
                cells,
                lax.ppermute(head, axis, [((i + 1) % count, i) for i in range(ends)]),
            ],
            axis=dim,
        )
    return cells


def dft_tables(width):
    indices = jnp.arange(width, dtype=jnp.int32)
    phases = indices[:, None] * indices[None, :] % width
    angles = phases.astype(jnp.float32) * (2.0 * math.pi / width)
    factor = 1.0 / math.sqrt(width)
    return (jnp.cos(angles) * factor, jnp.sin(angles) * factor)


def matrix_dot(first, second):
    return jnp.dot(first, second, precision=precision_mode, preferred_element_type=jnp.float32)


def complex_dot(first, second):
    real_part = matrix_dot(first[0], second[0]) - matrix_dot(first[1], second[1])
    imag_part = matrix_dot(first[0], second[1]) + matrix_dot(first[1], second[0])
    return (real_part, imag_part)


def fourier(field, tables, direction):
    matrix = (tables[0], direction * tables[1])
    return complex_dot(complex_dot(matrix, field), matrix)


def complex_mul(first, second):
    return (
        first[0] * second[0] - first[1] * second[1],
        first[0] * second[1] + first[1] * second[0],
    )


def conj_mul(first, second):
    return (
        first[0] * second[0] + first[1] * second[1],
        first[0] * second[1] - first[1] * second[0],
    )


def slot_gradient(patch, probe_wave, propagator, target, tables):
    layers = patch.shape[0]
    kernel = (propagator[0], propagator[1])
    wave = (probe_wave[0], probe_wave[1])
    incoming = []
    for layer_at in range(layers):
        incoming.append(wave)
        exited = complex_mul(wave, (patch[layer_at, 0], patch[layer_at, 1]))
        if layer_at + 1 < layers:
            wave = fourier(complex_mul(kernel, fourier(exited, tables, -1.0)), tables, 1.0)
    far_field = fourier(exited, tables, -1.0)
    misfit = far_field[0] * far_field[0] + far_field[1] * far_field[1] - target
    adjoint = fourier((misfit * far_field[0], misfit * far_field[1]), tables, 1.0)
    gradients = [None] * layers
    for layer_at in range(layers - 1, -1, -1):
        gradients[layer_at] = jnp.stack(conj_mul(incoming[layer_at], adjoint))
        adjoint = conj_mul((patch[layer_at, 0], patch[layer_at, 1]), adjoint)
        if layer_at > 0:
            adjoint = fourier(conj_mul(kernel, fourier(adjoint, tables, -1.0)), tables, 1.0)
    return (jnp.stack(gradients), jnp.stack(adjoint))


def add_block(base, block, row_start, col_start):
    return base.at[
        :, :, row_start : row_start + block.shape[2], col_start : col_start + block.shape[3]
    ].add(block)


def on_device(object_slices, probe_wave, propagator, measured, positions, scan_counts):
    layers = object_slices.shape[0]
    tile = object_slices.shape[2]
    width = probe_wave.shape[1]
    half = width // 2
    slots = measured.shape[2]
    tables = dft_tables(width)
    extended = padded(object_slices, (("row", 2), ("col", 3)), half)
    count = scan_counts[0, 0]
    valid = (jnp.arange(slots, dtype=jnp.int32) < count).astype(jnp.float32)
    local_total = jnp.sum(valid * jnp.sum(measured[0, 0], axis=(1, 2)))
    local_count = count.astype(jnp.float32)
    total, scans = lax.psum((local_total, local_count), ("row", "col"))

    def slot_starts(slot_at):
        offset = lax.dynamic_index_in_dim(positions[0, 0], slot_at, 0, keepdims=False)
        return (jnp.int32(0), jnp.int32(0), offset[0] + half, offset[1] + half)

    def visit(slot_at, state_pair):
        grad_ext, probe_sum = state_pair
        starts = slot_starts(slot_at)
        patch = lax.dynamic_slice(extended, starts, (layers, 2, width, width))
        target = lax.dynamic_index_in_dim(measured[0, 0], slot_at, 0, keepdims=False)
        gradients, adjoint = slot_gradient(patch, probe_wave, propagator, target, tables)
        region = lax.dynamic_slice(grad_ext, starts, (layers, 2, width, width)) + gradients
        grad_ext = lax.dynamic_update_slice(grad_ext, region, starts)
        return (grad_ext, probe_sum + adjoint)

    initial = (jnp.zeros_like(extended), jnp.zeros((2, width, width), jnp.float32))
    grad_ext, probe_sum = lax.fori_loop(0, count, visit, initial)
    edge_far = tile + half
    strips = jnp.concatenate((grad_ext[:, :, :half, :], grad_ext[:, :, edge_far:, :]), axis=2)
    rows_in = padded(strips, (("row", 2),), half)
    middle = grad_ext[:, :, half:edge_far, :]
    middle = add_block(middle, rows_in[:, :, :half, :], 0, 0)
    middle = add_block(middle, rows_in[:, :, 3 * half :, :], tile - half, 0)
    strips = jnp.concatenate((middle[:, :, :, :half], middle[:, :, :, edge_far:]), axis=3)
    cols_in = padded(strips, (("col", 3),), half)
    owned = middle[:, :, :, half:edge_far]
    owned = add_block(owned, cols_in[:, :, :, :half], 0, 0)
    owned = add_block(owned, cols_in[:, :, :, 3 * half :], 0, tile - half)
    probe_all = lax.psum(probe_sum, ("row", "col"))
    mean_level = total / (scans * (width * width))
    return (owned / mean_level, probe_all / (mean_level * scans))


def solution(mesh):
    placed = (
        P(None, None, "row", "col"),
        P(),
        P(),
        P("row", "col", None, None, None),
        P("row", "col", None, None),
        P("row", "col"),
    )
    return jax.shard_map(
        on_device,
        mesh=mesh,
        in_specs=placed,
        out_specs=(P(None, None, "row", "col"), P()),
        check_vma=False,
    )
```

profile of v0, /device:TPU:0, one launch (start us, length us, event | category | flops | bytes accessed | tf_op | source)
XLA Modules:
  0.0 650.6 jit_solution(11558558062728006596)
XLA Ops:
  8.6 2.4 collective-permute-start
  12.6 4.3 collective-permute-done.1
  18.1 4.4 collective-permute-start.2
  23.8 14.9 %collective-permute-done.2 = f32[2,2,512,128]{3,2,1,0:T(8,128)} collective-permute-done((f32[2,2,512,128]{3,2,1,0:T(8,128)}, f32[2,2,512,128]{3,2,1,0:T(8,128)}, u32[]{:S(2)}, u32[]{:S(2)}) %collective-permute-start.2) | collective-permute-done | bytes 1048608 | tf_op jit(solution)/shard_map/ppermute | solution.py:19
  38.7 24.8 %collective-permute-done.3 = f32[2,2,512,128]{3,2,1,0:T(8,128)} collective-permute-done((f32[2,2,512,128]{3,2,1,0:T(8,128)S(1)}, f32[2,2,512,128]{3,2,1,0:T(8,128)}, u32[]{:S(2)}, u32[]{:S(2)}) %collective-permute-start.3) | collective-permute-done | bytes 1048608 | tf_op jit(solution)/shard_map/ppermute | solution.py:21
  63.5 3.9 pad_maximum_fusion
  67.4 2.5 broadcast_in_dim.8
  70.0 99.3 %while.21 = (s32[]{:T(128)}, f32[2,2,512,512]{3,2,1,0:T(8,128)}, f32[2,256,256]{2,1,0:T(8,128)S(1)}, s32[]{:T(128)}, s32[1,1,4,2]{2,3,1,0:T(2,128)S(1)}, /*index...) while((s32[]{:T(128)}, f32[2,2,512,512]{3,2,1,0:T(8,128)}, ...), condition=%wide.region_1.2_spmd.clone.clone, body=%wide.region_0.1_spmd.clone.clone.sunk | while | flops 9717022720 | bytes 50332104 | solution.py:122
  85.7 3.1 fusion.449
  99.2 2.7 multiply_add_fusion.3
  112.4 1.7 fusion.456
  124.4 3.1 multiply_subtract_fusion.3
  137.9 2.7 fusion.463
  150.9 2.6 add_bitcast_fusion.3
  153.8 1.6 maximum_add_fusion.4
  155.4 9.4 %dynamic_update_slice.10 = f32[2,2,512,512]{3,2,1,0:T(8,128)} dynamic-update-slice(f32[2,2,512,512]{3,2,1,0:T(8,128)} %get-tuple-element.631, f32[2,2,256,256]{3,2,1,0:T(8,128)S(1)} %maximum_add_fusion.4, s32[]{:T(128)} %constant.177.clone.1..sunk, s32[]{:T(128)} %constant.177.clone.1..sunk, s32[]{:T(128)S(6)} %select_n.317, s32[]{:T(128)S(6)} %select_n.318) | dynamic-update-slice | bytes 2097156 | tf_op jit(solution)/shard_map/while/body/dynamic_update_slice | solution.py:118
  169.4 1.5 slice.230
  170.9 8.4 %collective-permute-start.4 = (f32[2,2,128,512]{3,2,1,0:T(8,128)S(1)}, f32[2,2,128,512]{3,2,1,0:T(8,128)S(1)}, u32[]{:S(2)}, u32[]{:S(2)}) collective-permute-start(f32[2,2,128,512]{3,2,1,0:T(8,128)S(1)} %slice.230), channel_id=1, source_target_pairs={{0,4},{4,8},{8,12},{12,16},{16,20},{20,24},{24,28},{1,5},{5,9},{9,... | collective-permute-start | bytes 3145736 | tf_op jit(solution)/shard_map/ppermute | solution.py:19
  179.3 1.8 slice.228
  183.2 18.9 %collective-permute-done.5 = f32[2,2,128,512]{3,2,1,0:T(8,128)S(1)} collective-permute-done((f32[2,2,128,512]{3,2,1,0:T(8,128)S(1)}, f32[2,2,128,512]{3,2,1,0:T(8,128)S(1)}, u32[]{:S(2)}, u32[]{:S(2)}) %collective-permute-start.5) | collective-permute-done | bytes 1048608 | tf_op jit(solution)/shard_map/ppermute | solution.py:21
  204.7 4.4 collective-permute-start.6
  211.9 349.4 %all-reduce = (f32[]{:T(128)}, f32[]{:T(128)}) all-reduce(f32[]{:T(128)} %fusion.272, f32[]{:T(128)S(6)} %convert_element_type.102), channel_id=1, replica_groups=mesh['row'=8,'col'=4] {'row','col'}, use_global_device_ids=true, to_apply=%region_4.5 | all-reduce | flops 2 | bytes 16 | tf_op jit(solution)/shard_map/psum | solution.py:105
  563.2 76.0 %all-reduce.3.cloned.1.call-done = f32[2,256,256]{2,1,0:T(8,128)} async-done(((f32[2,256,256]{2,1,0:T(8,128)}), f32[2,256,256]{2,1,0:T(8,128)}) %all-reduce.3.cloned.1.call-update) | async-done | bytes 524304 | tf_op jit(solution)/shard_map/psum | solution.py:134
  639.3 1.9 broadcast_divide_fusion.1
  (88 shorter events, 78.7 us)
Async XLA Ops:
  7.2 5.3 copy-start.5
  7.2 632.1 %all-reduce.3.cloned.1.call-start = ((), (), s32[]{:S(2)}) async-start(), calls=%async_computation | async-start | bytes 1048576 | tf_op jit(solution)/shard_map/psum | solution.py:134
  8.6 3.9 collective-permute-start
  11.0 6.0 collective-permute-start.1
  18.1 20.6 %collective-permute-start.2 = (f32[2,2,512,128]{3,2,1,0:T(8,128)}, f32[2,2,512,128]{3,2,1,0:T(8,128)}, u32[]{:S(2)}, u32[]{:S(2)}) collective-permute-start(f32[2,2,512,128]{3,2,1,0:T(8,128)} %get-tuple-element.507), channel_id=1, source_target_pairs={{0,1},{1,2},{2,3},{4,5},{5,6},{6,7},{8,9},{9,10},{10,11},{12,13},{... | collective-permute-start | bytes 3145736 | tf_op jit(solution)/shard_map/ppermute | solution.py:19
  22.5 41.0 %collective-permute-start.3 = (f32[2,2,512,128]{3,2,1,0:T(8,128)S(1)}, f32[2,2,512,128]{3,2,1,0:T(8,128)}, u32[]{:S(2)}, u32[]{:S(2)}) collective-permute-start(f32[2,2,512,128]{3,2,1,0:T(8,128)S(1)} %get-tuple-element.508), channel_id=1, source_target_pairs={{1,0},{2,1},{3,2},{5,4},{6,5},{7,6},{9,8},{10,9},{11,10},{13,12},{... | collective-permute-start | bytes 3145736 | tf_op jit(solution)/shard_map/ppermute | solution.py:21
  67.4 2.6 copy-start.1
  67.4 2.6 copy-start.6
  67.4 2.6 copy-start.7
  169.3 11.7 %copy-start.2 = (f32[2,256,256]{2,1,0:T(8,128)}, f32[2,256,256]{2,1,0:T(8,128)S(1)}, u32[]{:S(2)}) copy-start(f32[2,256,256]{2,1,0:T(8,128)S(1)} %get-tuple-element.359) | copy-start | bytes 1572868
  170.9 10.6 %copy-start = (f32[2,2,512,512]{3,2,1,0:T(8,128)S(1)}, f32[2,2,512,512]{3,2,1,0:T(8,128)}, u32[]{:S(2)}) copy-start(f32[2,2,512,512]{3,2,1,0:T(8,128)} %get-tuple-element.358) | copy-start | bytes 12582916
  170.9 10.6 %collective-permute-start.4 = (f32[2,2,128,512]{3,2,1,0:T(8,128)S(1)}, f32[2,2,128,512]{3,2,1,0:T(8,128)S(1)}, u32[]{:S(2)}, u32[]{:S(2)}) collective-permute-start(f32[2,2,128,512]{3,2,1,0:T(8,128)S(1)} %slice.230), channel_id=1, source_target_pairs={{0,4},{4,8},{8,12},{12,16},{16,20},{20,24},{24,28},{1,5},{5,9},{9,... | collective-permute-start | bytes 3145736 | tf_op jit(solution)/shard_map/ppermute | solution.py:19
  181.9 20.2 %collective-permute-start.5 = (f32[2,2,128,512]{3,2,1,0:T(8,128)S(1)}, f32[2,2,128,512]{3,2,1,0:T(8,128)S(1)}, u32[]{:S(2)}, u32[]{:S(2)}) collective-permute-start(f32[2,2,128,512]{3,2,1,0:T(8,128)S(1)} %get-tuple-element.503), channel_id=1, source_target_pairs={{4,0},{8,4},{12,8},{16,12},{20,16},{24,20},{28,24},{5,1},{9,5},{13... | collective-permute-start | bytes 3145736 | tf_op jit(solution)/shard_map/ppermute | solution.py:21
  202.4 1.3 copy-start.3
  204.7 436.4 %copy-start.4 = (f32[2,2,256,512]{3,2,1,0:T(8,128)S(1)}, f32[2,2,256,512]{3,2,1,0:T(8,128)}, u32[]{:S(2)}) copy-start(f32[2,2,256,512]{3,2,1,0:T(8,128)} %copy-done.3) | copy-start | bytes 6291460
  204.7 436.5 %collective-permute-start.6 = (f32[2,2,256,128]{3,2,1,0:T(8,128)}, f32[2,2,256,128]{3,2,1,0:T(8,128)}, u32[]{:S(2)}, u32[]{:S(2)}) collective-permute-start(f32[2,2,256,128]{3,2,1,0:T(8,128)} %get-tuple-element.506), channel_id=1, source_target_pairs={{0,1},{1,2},{2,3},{4,5},{5,6},{6,7},{8,9},{9,10},{10,11},{12,13},{... | collective-permute-start | bytes 1572872 | tf_op jit(solution)/shard_map/ppermute | solution.py:19
  210.0 432.4 %collective-permute-start.7 = (f32[2,2,256,128]{3,2,1,0:T(8,128)}, f32[2,2,256,128]{3,2,1,0:T(8,128)S(1)}, u32[]{:S(2)}, u32[]{:S(2)}) collective-permute-start(f32[2,2,256,128]{3,2,1,0:T(8,128)} %get-tuple-element.505), channel_id=1, source_target_pairs={{1,0},{2,1},{3,2},{5,4},{6,5},{7,6},{9,8},{10,9},{11,10},{13,12},{... | collective-permute-start | bytes 1572872 | tf_op jit(solution)/shard_map/ppermute | solution.py:21
Sparse Core Ops, SparseCore 0:
  209.2 429.9 all-reduce.2
where the time goes:
time: 654 us; the launch traced here: 651 us
  blocking collectives  349 us (53%)
  waiting for transfers between devices  140 us (21%)
  matrix products  77.9 us (12%)
  starting transfers between devices  24.7 us (4%)
  local copies, waits for them, and re-layouts  20.9 us (3%)
  between operations  17 us (3%)
  other arithmetic  12.7 us (2%)
  loops' own time  8.35 us (1%)
    psum x1, blocking collectives, on_device(): total, scans = lax.psum((local_total, local_count), ('row', 'col'))  349 us
    dot_general x48, matrix products, matrix_dot(): jnp.dot(first, second, precision=precision_mode, preferred_element_type=j...  77.9 us
    psum x1, waiting for transfers between devices, on_device(): probe_all = lax.psum(probe_sum, ('row', 'col'))  76 us
    ppermute x4, waiting for transfers between devices, padded(): lax.ppermute(head, axis, [((i + 1) % count, i) for i in range(ends)])  48.1 us
    ppermute x4, starting transfers between devices, padded(): lax.ppermute(tail, axis, [(i, (i + 1) % count) for i in range(ends)])  19.5 us
    ppermute x4, waiting for transfers between devices, padded(): lax.ppermute(tail, axis, [(i, (i + 1) % count) for i in range(ends)])  15.5 us
  transfers between devices with their start and end apart: 9, of which 7 were waited for; matrix products, arithmetic and copies ran while one was open for 1% of the time, Pallas kernels for 0%

commit v1 on v0

v1 whole, which is shorter than its diff:
```python
import functools

import jax
import jax.numpy as jnp
import numpy as np
from jax import lax
from jax.experimental import pallas as pl
from jax.experimental.pallas import tpu as pltpu
from jax.sharding import PartitionSpec as P

F32 = jnp.float32
BF16 = jnp.bfloat16


def split_table(table):
    high = table.astype(BF16)
    low = (table - high.astype(np.float64)).astype(BF16)
    return high, low


@functools.lru_cache(None)
def tables(width):
    half = width // 2
    index = np.arange(half)
    angle = 2.0 * np.pi * ((index[:, None] * index[None, :]) % half) / half
    cosine, sine = np.cos(angle) / np.sqrt(width), np.sin(angle) / np.sqrt(width)
    first = split_table(np.block([[cosine, sine], [-sine, cosine]]))
    second = split_table(np.block([[cosine, -sine], [sine, cosine]]))
    turn = 2.0 * np.pi * index / width
    turns = np.stack([np.cos(turn), np.sin(turn)]).astype(np.float32)
    row = np.broadcast_to(turns[:, :, None], (2, half, half))
    lane = np.broadcast_to(turns[:, None, :], (2, 8, half))
    spread = np.zeros((width, width))
    spread[np.arange(width), index_order(width)] = 1.0
    matrices = [*first, *second, spread.astype(BF16), spread.T.astype(BF16)]
    return np.stack(matrices), np.concatenate([row, lane], axis=1)


def index_order(width):
    index = np.arange(width)
    return index // 2 + (index % 2) * (width // 2)


def split(value):
    high = value.astype(BF16)
    low = (value - high.astype(F32)).astype(BF16)
    return high, low


def right_dot(value, matrix):
    high, low = split(value)
    return jnp.dot(
        jnp.concatenate([high, low, high], axis=1),
        jnp.concatenate([matrix[0], matrix[0], matrix[1]], axis=0),
        preferred_element_type=F32,
    )


def left_dot(matrix, value):
    high, low = split(value)
    return jnp.dot(
        jnp.concatenate([matrix[0], matrix[0], matrix[1]], axis=1),
        jnp.concatenate([high, low, high], axis=0),
        preferred_element_type=F32,
    )


def mul(a, b):
    return a[0] * b[0] - a[1] * b[1], a[0] * b[1] + a[1] * b[0]


def conj_mul(a, b):
    return a[0] * b[0] + a[1] * b[1], a[0] * b[1] - a[1] * b[0]


def right_forward(field, lane, matrix):
    half = field[0].shape[1] // 2
    rows = field[0].shape[0]
    a = tuple(part[:, :half] for part in field)
    b = tuple(part[:, half:] for part in field)
    u = (a[0] + b[0], a[1] + b[1])
    v = conj_mul(lane, (a[0] - b[0], a[1] - b[1]))
    stacked = jnp.concatenate(
        [jnp.concatenate(u, axis=1), jnp.concatenate(v, axis=1)], axis=0
    )
    out = right_dot(stacked, matrix)
    even, odd = out[:rows], out[rows:]
    return (
        jnp.concatenate([even[:, :half], odd[:, :half]], axis=1),
        jnp.concatenate([even[:, half:], odd[:, half:]], axis=1),
    )


def right_inverse(field, lane, matrix):
    half = field[0].shape[1] // 2
    rows = field[0].shape[0]
    even = jnp.concatenate([field[0][:, :half], field[1][:, :half]], axis=1)
    odd = jnp.concatenate([field[0][:, half:], field[1][:, half:]], axis=1)
    out = right_dot(jnp.concatenate([even, odd], axis=0), matrix)
    even, odd = out[:rows], out[rows:]
    even = (even[:, :half], even[:, half:])
    odd = mul(lane, (odd[:, :half], odd[:, half:]))
    return tuple(
        jnp.concatenate([e + o, e - o], axis=1) for e, o in zip(even, odd)
    )


def left_pair(field, row, forward, inverse, middle):
    half = field[0].shape[0] // 2
    lanes = field[0].shape[1]
    a = tuple(part[:half] for part in field)
    b = tuple(part[half:] for part in field)
    u = (a[0] + b[0], a[1] + b[1])
    v = conj_mul(row, (a[0] - b[0], a[1] - b[1]))
    stacked = jnp.concatenate(
        [jnp.concatenate(u, axis=0), jnp.concatenate(v, axis=0)], axis=1
    )
    out = left_dot(forward, stacked)
    even = middle(0, (out[:half, :lanes], out[half:, :lanes]))
    odd = middle(1, (out[:half, lanes:], out[half:, lanes:]))
    stacked = jnp.concatenate(
        [jnp.concatenate(even, axis=0), jnp.concatenate(odd, axis=0)], axis=1
    )
    out = left_dot(inverse, stacked)
    even = (out[:half, :lanes], out[half:, :lanes])
    odd = mul(row, (out[:half, lanes:], out[half:, lanes:]))
    return tuple(
        jnp.concatenate([e + o, e - o], axis=0) for e, o in zip(even, odd)
    )


def lane_pair(turns):
    half = turns.shape[2]
    return turns[0, half : half + 1, :], turns[1, half : half + 1, :]


def left_stage(works, turns, forward, inverse, middles):
    half = turns.shape[2]
    for at in range(works[0].shape[2] // half):
        lanes = pl.ds(at * half, half)
        for work, middle in zip(works, middles):
            out = left_pair(
                (work[0, :, lanes], work[1, :, lanes]),
                (turns[0, :half, :], turns[1, :half, :]),
                forward,
                inverse,
                functools.partial(middle, lanes),
            )
            work[0, :, lanes] = out[0]
            work[1, :, lanes] = out[1]


def pair_of(count, at):
    both = 2 * at + 1 < count
    second = 2 * at + both.astype(jnp.int32)
    return (2 * at, 1.0), (second, both.astype(F32))


def device_bits():
    row, col = lax.axis_index("row"), lax.axis_index("col")
    return row & 1, col & 1, (row >> 1) & 1, (row >> 2) & 1


def other_end(parity, span):
    return pl.multiple_of((1 - parity) * span, 8), pl.multiple_of(parity * span, 8)


def assemble(ext, bits, tile, sides, strips):
    half = sides[0].shape[2]
    size = tile.shape[1]
    blocks = size // half
    for part in range(2):
        for at in range(blocks):
            ext[part, 1 + at, half : half + size, :] = tile[part, :, at * half : (at + 1) * half]
        for side, at in zip(sides, ((1 - bits[1]) * (blocks + 1), bits[1] * (blocks + 1))):
            ext[part, at, half : half + size, :] = side[part]
        for strip, start in zip(strips, other_end(bits[0], half + size)):
            for at in range(blocks + 2):
                ext[part, at, pl.ds(start, half), :] = strip[part, :, at * half : (at + 1) * half]


def place(positions, slot_at, half):
    row = positions[0, slot_at] + half
    col = positions[1, slot_at] + half
    return row, col // half, col % half


def read_patch(ext, part, row, rows, base, shift, half):
    blocks = []
    for at in range(3):
        block = ext[part, base + at, pl.ds(row, rows), :]
        blocks.append(pltpu.roll(block, lax.rem(half - shift, half), 1))
    own = lax.broadcasted_iota(jnp.int32, (rows, half), 1) < half - shift
    return jnp.concatenate(
        [jnp.where(own, blocks[0], blocks[1]), jnp.where(own, blocks[1], blocks[2])], axis=1
    )


def add_patch(acc, part, row, base, shift, value):
    rows, width = value.shape
    half = width // 2
    first = pltpu.roll(value[:, :half], shift, 1)
    second = pltpu.roll(value[:, half:], shift, 1)
    own = lax.broadcasted_iota(jnp.int32, (rows, half), 1) >= shift
    zero = jnp.zeros_like(first)
    blocks = (
        jnp.where(own, first, zero),
        jnp.where(own, second, first),
        jnp.where(own, zero, second),
    )
    for at, block in enumerate(blocks):
        spot = (part, base + at, pl.ds(row, rows), slice(None))
        acc[spot] = acc[spot] + block


def write_out(acc, bits, centre, strips):
    half = acc.shape[3]
    size = centre.shape[1]
    for part in range(2):
        for at in range(centre.shape[2] // half):
            lanes = slice(at * half, (at + 1) * half)
            centre[part, :, lanes] = acc[part, at, half : half + size, :]
            for strip, start in zip(strips, other_end(bits[0], half + size)):
                strip[part, :, lanes] = acc[part, at, pl.ds(start, half), :]


CHUNK = 128


def chunks(width):
    return range(0, width, CHUNK)


def three_parts(value):
    high = value.astype(BF16)
    rest = value - high.astype(F32)
    middle = rest.astype(BF16)
    return high, middle, (rest - middle.astype(F32)).astype(BF16)


def prepare_kernel(count, measured, propagator, matrices, targets, kernel_out, total):
    slots = measured.shape[0]

    def reorder(source, at, out):
        moved = jnp.dot(
            jnp.concatenate(three_parts(source[at]), axis=1),
            jnp.concatenate([matrices[4]] * 3, axis=0),
            preferred_element_type=F32,
        )
        out[at] = jnp.dot(
            jnp.concatenate([matrices[5]] * 3, axis=1),
            jnp.concatenate(three_parts(moved), axis=0),
            preferred_element_type=F32,
        )

    used = jnp.float32(0.0)
    for slot_at in range(slots):
        reorder(measured, slot_at, targets)
        sums = jnp.sum(measured[slot_at])
        used = used + jnp.where(slot_at < count[0, 0], sums, jnp.float32(0.0))
    for part in range(2):
        reorder(propagator, part, kernel_out)
    total[0, 0] = used


def first_kernel(
    count, positions, tiles, side_a, side_b, strip_a, strip_b, probe, transfer,
    turns, matrices,
    waves, patches, ext, work,
):
    width = probe.shape[1]
    half = width // 2
    assemble(ext, device_bits(), tiles.at[0], (side_a, side_b), (strip_a, strip_b))

    def through(lanes, parity, value):
        rows = pl.ds(parity * half, half)
        return mul((transfer[0, rows, lanes], transfer[1, rows, lanes]), value)

    first, second = matrices.at[0:2], matrices.at[2:4]

    def visit(pair_at, carry):
        slots = [slot for slot, weight in pair_of(count[0, 0], pair_at)]
        places = [place(positions, slot, half) for slot in slots]
        works = [work.at[at] for at in range(2)]
        turn = lane_pair(turns)
        for at in chunks(width):
            rows = pl.ds(at, CHUNK)
            for slot, (row, base, shift), field in zip(slots, places, works):
                patch = tuple(
                    read_patch(ext, part, row + at, CHUNK, base, shift, half) for part in range(2)
                )
                for part in range(2):
                    patches[slot, part, rows, :] = patch[part]
                exited = mul((probe[0, rows, :], probe[1, rows, :]), patch)
                out = right_forward(exited, turn, second)
                field[0, rows, :] = out[0]
                field[1, rows, :] = out[1]
        left_stage(works, turns, first, second, [through] * 2)
        for at in chunks(width):
            rows = pl.ds(at, CHUNK)
            for slot, field in zip(slots, works):
                wave = right_inverse((field[0, rows, :], field[1, rows, :]), turn, first)
                waves[slot, 0, rows, :] = wave[0]
                waves[slot, 1, rows, :] = wave[1]
        return carry

    lax.fori_loop(0, (count[0, 0] + 1) // 2, visit, 0)


def second_kernel(
    count, positions, tiles, side_a, side_b, strip_a, strip_b, waves, targets,
    turns, matrices,
    backs, centre, send_a, send_b, ext, acc, patch, work,
):
    width = waves.shape[2]
    half = width // 2
    assemble(ext, device_bits(), tiles.at[1], (side_a, side_b), (strip_a, strip_b))
    acc[...] = jnp.zeros_like(acc)

    first, second = matrices.at[0:2], matrices.at[2:4]

    def visit(pair_at, carry):
        pair = pair_of(count[0, 0], pair_at)
        slots = [slot for slot, weight in pair]
        places = [place(positions, slot, half) for slot in slots]
        works = [work.at[at] for at in range(2)]
        turn = lane_pair(turns)

        def misfit(slot, lanes, parity, value):
            rows = pl.ds(parity * half, half)
            level = value[0] * value[0] + value[1] * value[1] - targets[slot, rows, lanes]
            return level * value[0], level * value[1]

        for at in chunks(width):
            rows = pl.ds(at, CHUNK)
            for which, (slot, (row, base, shift)) in enumerate(zip(slots, places)):
                cells = tuple(
                    read_patch(ext, part, row + at, CHUNK, base, shift, half) for part in range(2)
                )
                for part in range(2):
                    patch[which, part, rows, :] = cells[part]
                exited = mul((waves[slot, 0, rows, :], waves[slot, 1, rows, :]), cells)
                out = right_forward(exited, turn, second)
                works[which][0, rows, :] = out[0]
                works[which][1, rows, :] = out[1]
        left_stage(works, turns, first, second, [functools.partial(misfit, slot) for slot in slots])
        for at in chunks(width):
            rows = pl.ds(at, CHUNK)
            for which, ((slot, weight), (row, base, shift)) in enumerate(zip(pair, places)):
                field = works[which]
                adjoint = right_inverse((field[0, rows, :], field[1, rows, :]), turn, first)
                wave = (waves[slot, 0, rows, :], waves[slot, 1, rows, :])
                term = conj_mul(wave, adjoint)
                for part in range(2):
                    add_patch(acc, part, row + at, base, shift, term[part] * weight)
                back = conj_mul((patch[which, 0, rows, :], patch[which, 1, rows, :]), adjoint)
                out = right_forward(back, turn, second)
                backs[slot, 0, rows, :] = out[0]
                backs[slot, 1, rows, :] = out[1]
        return carry

    lax.fori_loop(0, (count[0, 0] + 1) // 2, visit, 0)
    write_out(acc, device_bits(), centre, (send_a, send_b))


def third_kernel(
    count, positions, used, patches, backs, probe, transfer,
    turns, matrices,
    adjoints, keep, send, work, probe_sum,
):
    width = probe.shape[1]
    half = width // 2
    probe_sum[...] = jnp.zeros_like(probe_sum)

    def through(lanes, parity, value):
        rows = pl.ds(parity * half, half)
        return conj_mul((transfer[0, rows, lanes], transfer[1, rows, lanes]), value)

    first, second = matrices.at[0:2], matrices.at[2:4]

    def visit(pair_at, carry):
        pair = pair_of(count[0, 0], pair_at)
        turn = lane_pair(turns)
        works = [work.at[at] for at in range(2)]
        for (slot, weight), own in zip(pair, works):
            own[...] = backs[slot]
        left_stage(works, turns, first, second, [through] * 2)
        for at in chunks(width):
            rows = pl.ds(at, CHUNK)
            for field, (slot, weight) in zip(works, pair):
                adjoint = right_inverse((field[0, rows, :], field[1, rows, :]), turn, first)
                cells = (patches[slot, 0, rows, :], patches[slot, 1, rows, :])
                back = conj_mul(cells, adjoint)
                for part in range(2):
                    adjoints[slot, part, rows, :] = adjoint[part]
                    probe_sum[part, rows, :] = probe_sum[part, rows, :] + back[part] * weight
        return carry

    lax.fori_loop(0, (count[0, 0] + 1) // 2, visit, 0)
    mine = device_bits()[0]
    keep[:width, :] = probe_sum[mine]
    send[:width, :] = probe_sum[1 - mine]
    scalars = jnp.where(
        lax.broadcasted_iota(jnp.int32, (SCALARS, width), 0) < SCALARS // 2,
        jnp.full((SCALARS, width), used[0, 0], F32),
        jnp.full((SCALARS, width), count[0, 0].astype(F32), F32),
    )
    keep[width:, :] = scalars
    send[width:, :] = scalars


def fourth_kernel(count, positions, probe, adjoints, centre, send_a, send_b, acc):
    width = probe.shape[1]
    half = width // 2
    acc[...] = jnp.zeros_like(acc)

    def visit(slot_at, carry):
        row, base, shift = place(positions, slot_at, half)
        for at in chunks(width):
            rows = pl.ds(at, CHUNK)
            adjoint = (adjoints[slot_at, 0, rows, :], adjoints[slot_at, 1, rows, :])
            term = conj_mul((probe[0, rows, :], probe[1, rows, :]), adjoint)
            for part in range(2):
                add_patch(acc, part, row + at, base, shift, term[part])
        return carry

    lax.fori_loop(0, count[0, 0], visit, 0)
    write_out(acc, device_bits(), centre, (send_a, send_b))


def edges_kernel(tiles, *outs):
    bits = device_bits()
    half = outs[0].shape[2]
    for at in range(tiles.shape[0]):
        for out, start in zip(outs[2 * at : 2 * at + 2], other_end(bits[1], tiles.shape[3] - half)):
            out[...] = tiles[at, :, :, pl.ds(pl.multiple_of(start, half), half)]


def widen_kernel(at, tiles, side_a, side_b, strip_a, strip_b):
    bits = device_bits()
    half = side_a.shape[2]
    size = tiles.shape[3]
    sides = other_end(bits[1], half + size)
    for out, start in zip((strip_a, strip_b), other_end(bits[0], size - half)):
        rows = pl.ds(start, half)
        out[:, :, half : half + size] = tiles[at, :, rows, :]
        for side, lane in zip((side_a, side_b), sides):
            out[:, :, pl.ds(pl.multiple_of(lane, half), half)] = side[:, rows, :]


def by_parity(bit, work):
    @pl.when(bit == 0)
    def _():
        work(1, 0)

    @pl.when(bit == 1)
    def _():
        work(0, 1)


def rows_kernel(centre, strip_a, strip_b, owned, side_a, side_b):
    bits = device_bits()
    half = strip_a.shape[1]
    size = centre.shape[1]
    strips, sides = (strip_a, strip_b), (side_a, side_b)

    def add(above, below):
        def part_sides(before, after):
            for out, lanes in (
                (sides[before], slice(0, half)),
                (owned, slice(half, half + size)),
                (sides[after], slice(half + size, 2 * half + size)),
            ):
                out[:, :half, :] = centre[:, :half, lanes] + strips[above][:, :, lanes]
                if size > 2 * half:
                    out[:, half : size - half, :] = centre[:, half : size - half, lanes]
                out[:, size - half :, :] = centre[:, size - half :, lanes] + strips[below][:, :, lanes]

        by_parity(bits[1], part_sides)

    by_parity(bits[0], add)


def mean_factor(scalars, width):
    scans = scalars[SCALARS // 2 : SCALARS // 2 + 1, :]
    return scans * float(width * width) / scalars[0:1, :], scans


def finish_object_kernel(scalars, *refs):
    *sources, object_grad = refs
    factor, scans = mean_factor(scalars, scalars.shape[1])
    lanes = object_grad.shape[3]

    def add(before, after):
        for at in range(object_grad.shape[0]):
            owned = sources[3 * at]
            sides = sources[3 * at + 1 : 3 * at + 3]
            half = sides[0].shape[2]
            scale = factor[:, :half][None]
            object_grad[at, :, :, :half] = (owned[:, :, :half] + sides[before][...]) * scale
            for start in range(half, lanes - half, half):
                object_grad[at, :, :, start : start + half] = owned[:, :, start : start + half] * scale
            object_grad[at, :, :, lanes - half :] = (
                owned[:, :, lanes - half :] + sides[after][...]
            ) * scale

    by_parity(device_bits()[1], add)


def finish_probe_kernel(scalars, own, other, probe_grad):
    factor, scans = mean_factor(scalars, scalars.shape[1])
    factor = factor / scans
    core = device_bits()[0]
    probe_grad[core] = own[...] * factor
    probe_grad[1 - core] = other[...] * factor


def add_kernel(*refs):
    *terms, out = refs
    total = terms[0][...]
    for term in terms[1:]:
        total = total + term[...]
    out[...] = total


def halve_kernel(which, kept, received, keep, send):
    bits = device_bits()
    rows = keep.shape[0] - SCALARS

    def part(first, second):
        for out, start in ((keep, first * rows), (send, second * rows)):
            out[:rows, :] = kept[start : start + rows, :] + received[start : start + rows, :]
            out[rows:, :] = kept[2 * rows :, :] + received[2 * rows :, :]

    by_parity(1 - bits[which], part)


def join_kernel(*refs):
    bits = device_bits()
    *pieces, out = refs
    rows = pieces[0].shape[0]
    for at, piece in enumerate(pieces):
        spot = (bits[2] ^ (at >> 1)) * 2 + (bits[3] ^ (at & 1))
        out[pl.ds(pl.multiple_of(spot * rows, rows), rows), :] = piece[...]


SCALARS = 8

SMEM = pl.BlockSpec(memory_space=pltpu.SMEM)
VMEM = pl.BlockSpec(memory_space=pltpu.VMEM)


def call(kernel, outs, scratch, scalars, arrays, cost, name, out_specs=None):
    moved = sum(4 * array.size for array in arrays)
    limit = (20 if scratch else 10) * 1024 * 1024
    return pl.pallas_call(
        kernel,
        out_shape=[jax.ShapeDtypeStruct(shape, F32) for shape in outs],
        in_specs=[SMEM] * len(scalars) + [VMEM] * len(arrays),
        out_specs=out_specs or [VMEM] * len(outs),
        scratch_shapes=[pltpu.VMEM(shape, F32) for shape in scratch],
        compiler_params=pltpu.CompilerParams(vmem_limit_bytes=limit),
        cost_estimate=pl.CostEstimate(flops=cost * 10**9, bytes_accessed=moved, transcendentals=0),
        name=name,
    )(*scalars, *arrays)


def swap(value, axis, bit):
    return lax.ppermute(value, axis, [(i, i ^ bit) for i in range(lax.axis_size(axis))])


def swap_next(value, axis):
    odd = range(1, lax.axis_size(axis) - 1, 2)
    return lax.ppermute(value, axis, [pair for i in odd for pair in ((i, i + 1), (i + 1, i))])


def both_swaps(values, axis):
    return [swap(values[0], axis, 1), swap_next(values[1], axis)]


def higher_bits(axis, bit):
    while bit < lax.axis_size(axis):
        yield bit
        bit *= 2


def on_device(object_slices, probe, propagator, measured, positions, scan_counts):
    layers = object_slices.shape[0]
    tile = object_slices.shape[2]
    width = probe.shape[1]
    half = width // 2
    slots = measured.shape[2]
    long = 2 * half + tile
    matrices, turns = (jnp.asarray(value) for value in tables(width))
    transforms = [turns, matrices]
    fields = (slots, 2, width, width)
    side, strip, middle = (2, tile, half), (2, half, long), (2, tile, long)
    wide, one = (2, 3 + tile // half, long, half), (2, width, width)
    two = (2, *one)
    places = positions[0, 0].T

    edges = call(edges_kernel, [side] * (2 * layers), [], [], [object_slices], 0, "tile_edges")
    sides = [both_swaps(edges[2 * at : 2 * at + 2], "col") for at in range(layers)]
    targets, transfer, used = call(
        prepare_kernel, [(slots, width, width), one, (1, 1)], [], [scan_counts],
        [measured[0, 0], propagator, matrices],
        6, "reorder_targets", [VMEM, VMEM, SMEM],
    )
    sides[0], targets, transfer = lax.optimization_barrier((sides[0], targets, transfer))
    strips = []
    for at in range(layers):
        pair = call(
            functools.partial(widen_kernel, at), [strip, strip], [], [],
            [object_slices, *sides[at]], 20, "widen",
        )
        strips.append(both_swaps(pair, "row"))

    waves, patches = call(
        first_kernel, [fields, fields], [wide, two], [scan_counts, places],
        [object_slices, *sides[0], *strips[0], probe, transfer, *transforms], 20, "first_slice",
    )
    backs, centre, *ends = call(
        second_kernel, [fields, middle, strip, strip], [wide, wide, two, two], [scan_counts, places],
        [object_slices, *sides[1], *strips[1], waves, targets, *transforms], 20, "second_slice",
    )

    def add_rows(centre, ends, cost=20):
        return call(
            rows_kernel, [(2, tile, tile), side, side], [], [], [centre, *ends], cost, "add_rows"
        )

    def halve(which, kept, received, cost=0):
        half_shape = ((kept.shape[0] - SCALARS) // 2 + SCALARS, width)
        return call(
            functools.partial(halve_kernel, which), [half_shape, half_shape], [], [],
            [kept, received], cost, "halve",
        )

    ends_last, centre_last = both_swaps(ends, "row"), centre
    message = (width + SCALARS, width)
    adjoints, keep, send = call(
        third_kernel, [fields, message, message], [two, one], [scan_counts, places, used],
        [patches, backs, probe, transfer, *transforms], 20, "first_adjoint",
    )
    keep, send = halve(2, keep, swap(send, "row", 1))
    send, ends_last = lax.optimization_barrier((send, ends_last))
    owned_last, *sides_last = add_rows(centre_last, ends_last)
    sides_last = both_swaps(sides_last, "col")
    keep, send = halve(3, keep, swap(send, "row", 2), 20)
    send, adjoints = lax.optimization_barrier((send, adjoints))
    centre, *ends = call(
        fourth_kernel, [middle, strip, strip], [wide], [scan_counts, places],
        [probe, adjoints], 20, "first_gradient",
    )
    ends = both_swaps(ends, "row")
    (state,) = call(
        add_kernel, [keep.shape], [], [], [keep, swap(send, "row", 4)], 20, "add",
    )
    ends, sides_last = lax.optimization_barrier((ends, sides_last))
    owned_first, *sides_first = add_rows(centre, ends)
    sides_first = both_swaps(sides_first, "col")
    (state,) = call(add_kernel, [state.shape], [], [], [state, swap(state, "col", 1)], 20, "add")
    (state,) = call(add_kernel, [state.shape], [], [], [state, swap(state, "col", 2)], 0, "add")
    for axis, bit in (("col", 4), ("row", 8)):
        for bit in higher_bits(axis, bit):
            state = state + swap(state, axis, bit)
    scalars, mine = state[-SCALARS:], state[:-SCALARS]
    (own,) = call(
        join_kernel, [(width, width)], [], [],
        [mine, *(swap(mine, "row", bit) for bit in (4, 2, 6))], 0, "join",
    )
    other = swap(own, "row", 1)
    (object_grad,) = call(
        finish_object_kernel, [object_slices.shape], [], [],
        [scalars, owned_first, *sides_first, owned_last, *sides_last], 20, "finish_object",
    )
    other, object_grad = lax.optimization_barrier((other, object_grad))
    (probe_grad,) = call(finish_probe_kernel, [one], [], [], [scalars, own, other], 0, "finish_probe")
    return object_grad, probe_grad


def solution(mesh):
    placed = (
        P(None, None, "row", "col"),
        P(),
        P(),
        P("row", "col", None, None, None),
        P("row", "col", None, None),
        P("row", "col"),
    )
    return jax.shard_map(
        on_device,
        mesh=mesh,
        in_specs=placed,
        out_specs=(P(None, None, "row", "col"), P()),
        check_vma=False,
    )
```

time: 654 us -> 99.5 us (0.15)
  blocking collectives: 349 us -> 0 us
  waiting for transfers between devices: 140 us -> 20.3 us
  matrix products: 77.9 us -> 0 us
  Pallas kernels: 0 us -> 25.7 us
  starting transfers between devices: 24.7 us -> 47 us
  local copies, waits for them, and re-layouts: 20.9 us -> 4.65 us
  between operations: 17 us -> 1.69 us
  other arithmetic: 12.7 us -> 0 us
  loops' own time: 8.35 us -> 0 us
    psum x1 -> x0, blocking collectives: 349 us -> none  [on_device(): total, scans = lax.psum((local_total, local_count), ('row', 'col'))]
    dot_general x48 -> x0, matrix products: 77.9 us -> none  [matrix_dot(): jnp.dot(first, second, precision=precision_mode, preferred_element_type=j...]
    psum x1 -> x0, waiting for transfers between devices: 76 us -> none  [on_device(): probe_all = lax.psum(probe_sum, ('row', 'col'))]
    ppermute x8 -> x25, waiting for transfers between devices: 63.6 us -> 20.3 us  [the longest x17 20.3 us: swap(): lax.ppermute(value, axis, [(i, i ^ bit) for i in range(lax.axis_size(axis...]
    pallas_call x0 -> x18, Pallas kernels: none -> 25.7 us  [call(): pl.pallas_call(kernel, out_shape=[jax.ShapeDtypeStruct(shape, F32) for sh...]
    ppermute x8 -> x25, starting transfers between devices: 24.7 us -> 47 us  [the longest x17 41.4 us: swap(): lax.ppermute(value, axis, [(i, i ^ bit) for i in range(lax.axis_size(axis...]
    dynamic_update_slice x1 -> x0, local copies, waits for them, and re-layouts: 9.4 us -> none  [visit(): grad_ext = lax.dynamic_update_slice(grad_ext, region, starts)]
    another operation x1 -> x0, loops' own time: 8.35 us -> none  [on_device(): grad_ext, probe_sum = lax.fori_loop(0, count, visit, initial)]
  transfers between devices with their start and end apart: 9 -> 25, of which waited for: 7 -> 8; matrix products, arithmetic and copies ran while one was open for 1% -> 0% of each run, Pallas kernels for 0% -> 17%
where the time goes in v1:
time: 99.5 us; the launch traced here: 99.3 us
  starting transfers between devices  47 us (47%)
  Pallas kernels  25.7 us (26%)
  waiting for transfers between devices  20.3 us (20%)
  local copies, waits for them, and re-layouts  4.65 us (5%)
  between operations  1.69 us (2%)
    ppermute x17, starting transfers between devices, swap(): lax.ppermute(value, axis, [(i, i ^ bit) for i in range(lax.axis_size(axis...  41.4 us
    pallas_call x18, Pallas kernels, call(): pl.pallas_call(kernel, out_shape=[jax.ShapeDtypeStruct(shape, F32) for sh...  25.7 us
    ppermute x17, waiting for transfers between devices, swap(): lax.ppermute(value, axis, [(i, i ^ bit) for i in range(lax.axis_size(axis...  20.3 us
    ppermute x8, starting transfers between devices, swap_next(): lax.ppermute(value, axis, [pair for i in odd for pair in ((i, i + 1), (i...  5.56 us
    unnamed x18, local copies, waits for them, and re-layouts  4.64 us
  transfers between devices with their start and end apart: 25, of which 8 were waited for; matrix products, arithmetic and copies ran while one was open for 0% of the time, Pallas kernels for 17%

profile of v1, /device:TPU:0, one launch (start us, length us, event | category | flops | bytes accessed | tf_op | source)
XLA Modules:
  0.0 99.3 jit_solution(17638465350563655586)
XLA Ops:
  0.6 1.2 %copy-done = f32[2,2,256,256]{3,2,1,0:T(8,128)S(1)} copy-done((f32[2,2,256,256]{3,2,1,0:T(8,128)S(1)}, f32[2,2,256,256]{3,2,1,0:T(8,128)}, u32[]{:S(2)}) %copy-start) | copy-done | bytes 1048600
  1.9 3.0 %collective-permute-start = (f32[2,256,128]{2,1,0:T(8,128)S(1)}, f32[2,256,128]{2,1,0:T(8,128)S(1)}, u32[]{:S(2)}, u32[]{:S(2)}) collective-permute-start(f32[2,256,128]{2,1,0:T(8,128)S(1)} %get-tuple-element.51), channel_id=1, source_target_pairs={{0,1},{1,0},{2,3},{3,2},{4,5},{5,4},{6,7},{7,6},{8,9},{9,8},{10,11... | collective-permute-start | bytes 786440 | tf_op jit(solution)/shard_map/ppermute | solution.py:569
  5.6 4.3 %collective-permute-start.4 = (f32[2,256,128]{2,1,0:T(8,128)S(1)}, f32[2,256,128]{2,1,0:T(8,128)S(1)}, u32[]{:S(2)}, u32[]{:S(2)}) collective-permute-start(f32[2,256,128]{2,1,0:T(8,128)S(1)} %get-tuple-element.61), channel_id=1, source_target_pairs={{0,1},{1,0},{2,3},{3,2},{4,5},{5,4},{6,7},{7,6},{8,9},{9,8},{10,11... | collective-permute-start | bytes 786440 | tf_op jit(solution)/shard_map/ppermute | solution.py:569
  11.2 1.2 %copy-done.2 = f32[1,1,4,256,256]{4,3,2,1,0:T(8,128)S(1)} copy-done((f32[1,1,4,256,256]{4,3,2,1,0:T(8,128)S(1)}, f32[1,1,4,256,256]{4,3,2,1,0:T(8,128)}, u32[]{:S(2)}) %copy-start.2) | copy-done | bytes 1048600
  14.6 2.2 %reorder_targets.1 = (f32[4,256,256]{2,1,0:T(8,128)S(1)}, f32[2,256,256]{2,1,0:T(8,128)S(1)}, f32[1,1]{1,0:T(1,128)}) custom-call(s32[1,1]{1,0:T(1,128)S(6)} %copy.10.count, f32[4,256,256]{2,1,0:T(8,128)S(1)} %bitcast.4, f32[2,256,256]{2,1,0:T(8,128)S(1)} %copy-done.3, bf16[6,256,256]{2,1,0:T(8,128)(2,1)S(1)} %copy-done.6), custom_call_target="tpu_custom_call" | custom-call | flops 6000000000 | bytes 3145728 | tf_op jit(solution)/shard_map/reorder_targets/pallas_call | solution.py:556
  17.9 5.4 %collective-permute-done.4.side_a = f32[2,256,128]{2,1,0:T(8,128)S(1)} collective-permute-done((f32[2,256,128]{2,1,0:T(8,128)S(1)}, f32[2,256,128]{2,1,0:T(8,128)S(1)}, u32[]{:S(2)}, u32[]{:S(2)}) %collective-permute-start.4) | collective-permute-done | bytes 262176 | tf_op jit(solution)/shard_map/ppermute | solution.py:569
  24.3 5.9 %first_slice.1 = (f32[4,2,256,256]{3,2,1,0:T(8,128)S(1)}, f32[4,2,256,256]{3,2,1,0:T(8,128)S(1)}) custom-call(s32[1,1]{1,0:T(1,128)S(6)} %copy.10.count, s32[2,4]{1,0:T(2,128)S(1)} %bitcast.5, f32[2,2,256,256]{3,2,1,0:T(8,128)S(1)} %copy-done.1, f32[2,256,128]{2,1,0:T(8,128)S(1)} %collective-permute-done.side_a, ...), custom_call_target="tpu_custom_call" | custom-call | flops 20000000000 | bytes 5382144 | tf_op jit(solution)/shard_map/first_slice/pallas_call | solution.py:556
  30.2 7.7 %second_slice.1 = (f32[4,2,256,256]{3,2,1,0:T(8,128)S(1)}, f32[2,256,512]{2,1,0:T(8,128)S(1)}, f32[2,128,512]{2,1,0:T(8,128)S(1)}, f32[2,128,512]{2,1,0:T(8,128)S(1)}) custom-call(s32[1,1]{1,0:T(1,128)S(6)} %copy.10.count, s32[2,4]{1,0:T(2,128)S(1)} %bitcast.6, f32[2,2,256,256]{3,2,1,0:T(8,128)S(1)} %copy-done.1, ...), custom_call_target="tpu_custom_call" | custom-call | flops 20000000000 | bytes 7479296 | tf_op jit(solution)/shard_map/second_slice/pallas_call | solution.py:556
  37.9 4.3 %collective-permute-start.9 = (f32[2,128,512]{2,1,0:T(8,128)S(1)}, f32[2,128,512]{2,1,0:T(8,128)S(1)}, u32[]{:S(2)}, u32[]{:S(2)}) collective-permute-start(f32[2,128,512]{2,1,0:T(8,128)S(1)} %get-tuple-element.72), channel_id=1, source_target_pairs={{0,4},{4,0},{8,12},{12,8},{16,20},{20,16},{24,28},{28,24},{1,5},{5... | collective-permute-start | bytes 1572872 | tf_op jit(solution)/shard_map/ppermute | solution.py:569
  42.9 5.2 %first_adjoint.1 = (f32[4,2,256,256]{3,2,1,0:T(8,128)S(1)}, f32[264,256]{1,0:T(8,128)S(1)}, f32[264,256]{1,0:T(8,128)S(1)}) custom-call(s32[1,1]{1,0:T(1,128)S(6)} %copy.10.count, s32[2,4]{1,0:T(2,128)S(1)} %bitcast.7, f32[1,1]{1,0:T(1,128)} %get-tuple-element.50.used, f32[4,2,256,256]{3,2,1,0:T(8,128)S(1)} %get-tuple-element.60.patches, ...), custom_call_target="tpu_custom_call" | custom-call | flops 20000000000 | bytes 6955008 | tf_op jit(solution)/shard_map/first_adjoint/pallas_call | solution.py:556
  48.1 3.5 %collective-permute-start.8 = (f32[264,256]{1,0:T(8,128)S(1)}, f32[264,256]{1,0:T(8,128)S(1)}, u32[]{:S(2)}, u32[]{:S(2)}) collective-permute-start(f32[264,256]{1,0:T(8,128)S(1)} %get-tuple-element.69), channel_id=1, source_target_pairs={{0,4},{4,0},{8,12},{12,8},{16,20},{20,16},{24,28},{28,24},{1,5},{5... | collective-permute-start | bytes 811016 | tf_op jit(solution)/shard_map/ppermute | solution.py:569
  52.8 2.0 %collective-permute-start.11 = (f32[136,256]{1,0:T(8,128)S(1)}, f32[136,256]{1,0:T(8,128)S(1)}, u32[]{:S(2)}, u32[]{:S(2)}) collective-permute-start(f32[136,256]{1,0:T(8,128)S(1)} %get-tuple-element.74), channel_id=1, source_target_pairs={{0,8},{4,12},{8,0},{12,4},{16,24},{20,28},{24,16},{28,20},{1,9},{5... | collective-permute-start | bytes 417800 | tf_op jit(solution)/shard_map/ppermute | solution.py:569
  55.0 6.5 %collective-permute-start.21 = (f32[2,256,128]{2,1,0:T(8,128)S(1)}, f32[2,256,128]{2,1,0:T(8,128)S(1)}, u32[]{:S(2)}, u32[]{:S(2)}) collective-permute-start(f32[2,256,128]{2,1,0:T(8,128)S(1)} %get-tuple-element.86), channel_id=1, source_target_pairs={{0,1},{1,0},{2,3},{3,2},{4,5},{5,4},{6,7},{7,6},{8,9},{9,8},{10,11... | collective-permute-start | bytes 786440 | tf_op jit(solution)/shard_map/ppermute | solution.py:569
  62.3 1.4 %collective-permute-start.12 = (f32[72,256]{1,0:T(8,128)S(1)}, f32[72,256]{1,0:T(8,128)S(1)}, u32[]{:S(2)}, u32[]{:S(2)}) collective-permute-start(f32[72,256]{1,0:T(8,128)S(1)} %get-tuple-element.78), channel_id=1, source_target_pairs={{0,16},{4,20},{8,24},{12,28},{16,0},{20,4},{24,8},{28,12},{1,17},{... | collective-permute-start | bytes 221192 | tf_op jit(solution)/shard_map/ppermute | solution.py:569
  63.6 2.0 %first_gradient.1 = (f32[2,256,512]{2,1,0:T(8,128)S(1)}, f32[2,128,512]{2,1,0:T(8,128)S(1)}, f32[2,128,512]{2,1,0:T(8,128)S(1)}) custom-call(s32[1,1]{1,0:T(1,128)S(6)} %copy.10.count, s32[2,4]{1,0:T(2,128)S(1)} %bitcast.8, f32[2,256,256]{2,1,0:T(8,128)S(1)} %copy-done.4, f32[4,2,256,256]{3,2,1,0:T(8,128)S(1)} %get-tuple-element.79.adjoints), custom_call_target="tpu_custom_call" | custom-call | flops 20000000000 | bytes 2621440 | tf_op jit(solution)/shard_map/first_gradient/pallas_call | solution.py:556
  66.4 2.3 %collective-permute-done.12.refs_1_ = f32[72,256]{1,0:T(8,128)S(1)} collective-permute-done((f32[72,256]{1,0:T(8,128)S(1)}, f32[72,256]{1,0:T(8,128)S(1)}, u32[]{:S(2)}, u32[]{:S(2)}) %collective-permute-start.12) | collective-permute-done | bytes 73760 | tf_op jit(solution)/shard_map/ppermute | solution.py:569
  68.7 3.8 %collective-permute-start.13 = (f32[72,256]{1,0:T(8,128)S(1)}, f32[72,256]{1,0:T(8,128)S(1)}, u32[]{:S(2)}, u32[]{:S(2)}) collective-permute-start(f32[72,256]{1,0:T(8,128)S(1)} %add.3.refs_0_), channel_id=1, source_target_pairs={{0,1},{1,0},{2,3},{3,2},{4,5},{5,4},{6,7},{7,6},{8,9},{9,8},{10,11... | collective-permute-start | bytes 221192 | tf_op jit(solution)/shard_map/ppermute | solution.py:569
  72.7 2.2 %collective-permute-start.23 = (f32[2,256,128]{2,1,0:T(8,128)S(1)}, f32[2,256,128]{2,1,0:T(8,128)S(1)}, u32[]{:S(2)}, u32[]{:S(2)}) collective-permute-start(f32[2,256,128]{2,1,0:T(8,128)S(1)} %get-tuple-element.91), channel_id=1, source_target_pairs={{0,1},{1,0},{2,3},{3,2},{4,5},{5,4},{6,7},{7,6},{8,9},{9,8},{10,11... | collective-permute-start | bytes 786440 | tf_op jit(solution)/shard_map/ppermute | solution.py:569
  75.6 2.8 %collective-permute-start.14 = (f32[72,256]{1,0:T(8,128)S(1)}, f32[72,256]{1,0:T(8,128)S(1)}, u32[]{:S(2)}, u32[]{:S(2)}) collective-permute-start(f32[72,256]{1,0:T(8,128)S(1)} %add.4.refs_0_), channel_id=1, source_target_pairs={{0,2},{1,3},{2,0},{3,1},{4,6},{5,7},{6,4},{7,5},{8,10},{9,11},{10,... | collective-permute-start | bytes 221192 | tf_op jit(solution)/shard_map/ppermute | solution.py:569
  78.4 4.7 %collective-permute-done.14.refs_1_ = f32[72,256]{1,0:T(8,128)S(1)} collective-permute-done((f32[72,256]{1,0:T(8,128)S(1)}, f32[72,256]{1,0:T(8,128)S(1)}, u32[]{:S(2)}, u32[]{:S(2)}) %collective-permute-start.14) | collective-permute-done | bytes 73760 | tf_op jit(solution)/shard_map/ppermute | solution.py:569
  83.1 6.8 %collective-permute-start.17 = (f32[64,256]{1,0:T(8,128)S(1)}, f32[64,256]{1,0:T(8,128)S(1)}, u32[]{:S(2)}, u32[]{:S(2)}) collective-permute-start(f32[64,256]{1,0:T(8,128)S(1)} %slice.8.refs_0_), channel_id=1, source_target_pairs={{0,24},{4,28},{8,16},{12,20},{16,8},{20,12},{24,0},{28,4},{1,25},{... | collective-permute-start | bytes 196616 | tf_op jit(solution)/shard_map/ppermute | solution.py:569
  90.5 1.7 %collective-permute-done.17.refs_3_ = f32[64,256]{1,0:T(8,128)S(1)} collective-permute-done((f32[64,256]{1,0:T(8,128)S(1)}, f32[64,256]{1,0:T(8,128)S(1)}, u32[]{:S(2)}, u32[]{:S(2)}) %collective-permute-start.17) | collective-permute-done | bytes 65568 | tf_op jit(solution)/shard_map/ppermute | solution.py:569
  92.2 3.3 %collective-permute-done.16.refs_2_ = f32[64,256]{1,0:T(8,128)S(1)} collective-permute-done((f32[64,256]{1,0:T(8,128)S(1)}, f32[64,256]{1,0:T(8,128)S(1)}, u32[]{:S(2)}, u32[]{:S(2)}) %collective-permute-start.16) | collective-permute-done | bytes 65568 | tf_op jit(solution)/shard_map/ppermute | solution.py:569
  95.5 1.3 %collective-permute-done.15.refs_1_ = f32[64,256]{1,0:T(8,128)S(1)} collective-permute-done((f32[64,256]{1,0:T(8,128)S(1)}, f32[64,256]{1,0:T(8,128)S(1)}, u32[]{:S(2)}, u32[]{:S(2)}) %collective-permute-start.15) | collective-permute-done | bytes 65568 | tf_op jit(solution)/shard_map/ppermute | solution.py:569
  (64 shorter events, 13.1 us)
Async XLA Ops:
  1.9 14.9 %collective-permute-start = (f32[2,256,128]{2,1,0:T(8,128)S(1)}, f32[2,256,128]{2,1,0:T(8,128)S(1)}, u32[]{:S(2)}, u32[]{:S(2)}) collective-permute-start(f32[2,256,128]{2,1,0:T(8,128)S(1)} %get-tuple-element.51), channel_id=1, source_target_pairs={{0,1},{1,0},{2,3},{3,2},{4,5},{5,4},{6,7},{7,6},{8,9},{9,8},{10,11... | collective-permute-start | bytes 786440 | tf_op jit(solution)/shard_map/ppermute | solution.py:569
  4.9 11.9 %collective-permute-start.1 = (f32[2,256,128]{2,1,0:T(8,128)S(1)}, f32[2,256,128]{2,1,0:T(8,128)S(1)}, u32[]{:S(2)}, u32[]{:S(2)}) collective-permute-start(f32[2,256,128]{2,1,0:T(8,128)S(1)} %get-tuple-element.52), channel_id=1, source_target_pairs={{1,2},{2,1},{5,6},{6,5},{9,10},{10,9},{13,14},{14,13},{17,18},{18,... | collective-permute-start | bytes 786440 | tf_op jit(solution)/shard_map/ppermute | solution.py:574
  5.6 17.7 %collective-permute-start.4 = (f32[2,256,128]{2,1,0:T(8,128)S(1)}, f32[2,256,128]{2,1,0:T(8,128)S(1)}, u32[]{:S(2)}, u32[]{:S(2)}) collective-permute-start(f32[2,256,128]{2,1,0:T(8,128)S(1)} %get-tuple-element.61), channel_id=1, source_target_pairs={{0,1},{1,0},{2,3},{3,2},{4,5},{5,4},{6,7},{7,6},{8,9},{9,8},{10,11... | collective-permute-start | bytes 786440 | tf_op jit(solution)/shard_map/ppermute | solution.py:569
  9.9 13.4 %collective-permute-start.5 = (f32[2,256,128]{2,1,0:T(8,128)S(1)}, f32[2,256,128]{2,1,0:T(8,128)S(1)}, u32[]{:S(2)}, u32[]{:S(2)}) collective-permute-start(f32[2,256,128]{2,1,0:T(8,128)S(1)} %get-tuple-element.62), channel_id=1, source_target_pairs={{1,2},{2,1},{5,6},{6,5},{9,10},{10,9},{13,14},{14,13},{17,18},{18,... | collective-permute-start | bytes 786440 | tf_op jit(solution)/shard_map/ppermute | solution.py:574
  16.9 7.3 %collective-permute-start.2 = (f32[2,128,512]{2,1,0:T(8,128)S(1)}, f32[2,128,512]{2,1,0:T(8,128)S(1)}, u32[]{:S(2)}, u32[]{:S(2)}) collective-permute-start(f32[2,128,512]{2,1,0:T(8,128)S(1)} %get-tuple-element.57), channel_id=1, source_target_pairs={{0,4},{4,0},{8,12},{12,8},{16,20},{20,16},{24,28},{28,24},{1,5},{5... | collective-permute-start | bytes 1572872 | tf_op jit(solution)/shard_map/ppermute | solution.py:569
  17.1 7.1 %collective-permute-start.3 = (f32[2,128,512]{2,1,0:T(8,128)S(1)}, f32[2,128,512]{2,1,0:T(8,128)S(1)}, u32[]{:S(2)}, u32[]{:S(2)}) collective-permute-start(f32[2,128,512]{2,1,0:T(8,128)S(1)} %get-tuple-element.58), channel_id=1, source_target_pairs={{4,8},{8,4},{12,16},{16,12},{20,24},{24,20},{5,9},{9,5},{13,17},{1... | collective-permute-start | bytes 1572872 | tf_op jit(solution)/shard_map/ppermute | solution.py:574
  23.4 6.8 %collective-permute-start.6 = (f32[2,128,512]{2,1,0:T(8,128)S(1)}, f32[2,128,512]{2,1,0:T(8,128)S(1)}, u32[]{:S(2)}, u32[]{:S(2)}) collective-permute-start(f32[2,128,512]{2,1,0:T(8,128)S(1)} %get-tuple-element.63), channel_id=1, source_target_pairs={{0,4},{4,0},{8,12},{12,8},{16,20},{20,16},{24,28},{28,24},{1,5},{5... | collective-permute-start | bytes 1572872 | tf_op jit(solution)/shard_map/ppermute | solution.py:569
  23.5 6.7 %collective-permute-start.7 = (f32[2,128,512]{2,1,0:T(8,128)S(1)}, f32[2,128,512]{2,1,0:T(8,128)S(1)}, u32[]{:S(2)}, u32[]{:S(2)}) collective-permute-start(f32[2,128,512]{2,1,0:T(8,128)S(1)} %get-tuple-element.64), channel_id=1, source_target_pairs={{4,8},{8,4},{12,16},{16,12},{20,24},{24,20},{5,9},{9,5},{13,17},{1... | collective-permute-start | bytes 1572872 | tf_op jit(solution)/shard_map/ppermute | solution.py:574
  37.9 14.9 %collective-permute-start.9 = (f32[2,128,512]{2,1,0:T(8,128)S(1)}, f32[2,128,512]{2,1,0:T(8,128)S(1)}, u32[]{:S(2)}, u32[]{:S(2)}) collective-permute-start(f32[2,128,512]{2,1,0:T(8,128)S(1)} %get-tuple-element.72), channel_id=1, source_target_pairs={{0,4},{4,0},{8,12},{12,8},{16,20},{20,16},{24,28},{28,24},{1,5},{5... | collective-permute-start | bytes 1572872 | tf_op jit(solution)/shard_map/ppermute | solution.py:569
  42.2 10.7 %collective-permute-start.10 = (f32[2,128,512]{2,1,0:T(8,128)S(1)}, f32[2,128,512]{2,1,0:T(8,128)S(1)}, u32[]{:S(2)}, u32[]{:S(2)}) collective-permute-start(f32[2,128,512]{2,1,0:T(8,128)S(1)} %get-tuple-element.73), channel_id=1, source_target_pairs={{4,8},{8,4},{12,16},{16,12},{20,24},{24,20},{5,9},{9,5},{13,17},{1... | collective-permute-start | bytes 1572872 | tf_op jit(solution)/shard_map/ppermute | solution.py:574
  48.1 4.7 %collective-permute-start.8 = (f32[264,256]{1,0:T(8,128)S(1)}, f32[264,256]{1,0:T(8,128)S(1)}, u32[]{:S(2)}, u32[]{:S(2)}) collective-permute-start(f32[264,256]{1,0:T(8,128)S(1)} %get-tuple-element.69), channel_id=1, source_target_pairs={{0,4},{4,0},{8,12},{12,8},{16,20},{20,16},{24,28},{28,24},{1,5},{5... | collective-permute-start | bytes 811016 | tf_op jit(solution)/shard_map/ppermute | solution.py:569
  52.8 9.4 %collective-permute-start.11 = (f32[136,256]{1,0:T(8,128)S(1)}, f32[136,256]{1,0:T(8,128)S(1)}, u32[]{:S(2)}, u32[]{:S(2)}) collective-permute-start(f32[136,256]{1,0:T(8,128)S(1)} %get-tuple-element.74), channel_id=1, source_target_pairs={{0,8},{4,12},{8,0},{12,4},{16,24},{20,28},{24,16},{28,20},{1,9},{5... | collective-permute-start | bytes 417800 | tf_op jit(solution)/shard_map/ppermute | solution.py:569
  55.0 17.5 %collective-permute-start.21 = (f32[2,256,128]{2,1,0:T(8,128)S(1)}, f32[2,256,128]{2,1,0:T(8,128)S(1)}, u32[]{:S(2)}, u32[]{:S(2)}) collective-permute-start(f32[2,256,128]{2,1,0:T(8,128)S(1)} %get-tuple-element.86), channel_id=1, source_target_pairs={{0,1},{1,0},{2,3},{3,2},{4,5},{5,4},{6,7},{7,6},{8,9},{9,8},{10,11... | collective-permute-start | bytes 786440 | tf_op jit(solution)/shard_map/ppermute | solution.py:569
  61.5 11.0 %collective-permute-start.22 = (f32[2,256,128]{2,1,0:T(8,128)S(1)}, f32[2,256,128]{2,1,0:T(8,128)S(1)}, u32[]{:S(2)}, u32[]{:S(2)}) collective-permute-start(f32[2,256,128]{2,1,0:T(8,128)S(1)} %get-tuple-element.87), channel_id=1, source_target_pairs={{1,2},{2,1},{5,6},{6,5},{9,10},{10,9},{13,14},{14,13},{17,18},{18,... | collective-permute-start | bytes 786440 | tf_op jit(solution)/shard_map/ppermute | solution.py:574
  62.3 6.4 %collective-permute-start.12 = (f32[72,256]{1,0:T(8,128)S(1)}, f32[72,256]{1,0:T(8,128)S(1)}, u32[]{:S(2)}, u32[]{:S(2)}) collective-permute-start(f32[72,256]{1,0:T(8,128)S(1)} %get-tuple-element.78), channel_id=1, source_target_pairs={{0,16},{4,20},{8,24},{12,28},{16,0},{20,4},{24,8},{28,12},{1,17},{... | collective-permute-start | bytes 221192 | tf_op jit(solution)/shard_map/ppermute | solution.py:569
  65.6 6.9 %collective-permute-start.19 = (f32[2,128,512]{2,1,0:T(8,128)S(1)}, f32[2,128,512]{2,1,0:T(8,128)S(1)}, u32[]{:S(2)}, u32[]{:S(2)}) collective-permute-start(f32[2,128,512]{2,1,0:T(8,128)S(1)} %get-tuple-element.81), channel_id=1, source_target_pairs={{0,4},{4,0},{8,12},{12,8},{16,20},{20,16},{24,28},{28,24},{1,5},{5... | collective-permute-start | bytes 1572872 | tf_op jit(solution)/shard_map/ppermute | solution.py:569
  65.7 6.8 %collective-permute-start.20 = (f32[2,128,512]{2,1,0:T(8,128)S(1)}, f32[2,128,512]{2,1,0:T(8,128)S(1)}, u32[]{:S(2)}, u32[]{:S(2)}) collective-permute-start(f32[2,128,512]{2,1,0:T(8,128)S(1)} %get-tuple-element.82), channel_id=1, source_target_pairs={{4,8},{8,4},{12,16},{16,12},{20,24},{24,20},{5,9},{9,5},{13,17},{1... | collective-permute-start | bytes 1572872 | tf_op jit(solution)/shard_map/ppermute | solution.py:574
  68.7 6.9 %collective-permute-start.13 = (f32[72,256]{1,0:T(8,128)S(1)}, f32[72,256]{1,0:T(8,128)S(1)}, u32[]{:S(2)}, u32[]{:S(2)}) collective-permute-start(f32[72,256]{1,0:T(8,128)S(1)} %add.3.refs_0_), channel_id=1, source_target_pairs={{0,1},{1,0},{2,3},{3,2},{4,5},{5,4},{6,7},{7,6},{8,9},{9,8},{10,11... | collective-permute-start | bytes 221192 | tf_op jit(solution)/shard_map/ppermute | solution.py:569
  72.7 24.2 %collective-permute-start.23 = (f32[2,256,128]{2,1,0:T(8,128)S(1)}, f32[2,256,128]{2,1,0:T(8,128)S(1)}, u32[]{:S(2)}, u32[]{:S(2)}) collective-permute-start(f32[2,256,128]{2,1,0:T(8,128)S(1)} %get-tuple-element.91), channel_id=1, source_target_pairs={{0,1},{1,0},{2,3},{3,2},{4,5},{5,4},{6,7},{7,6},{8,9},{9,8},{10,11... | collective-permute-start | bytes 786440 | tf_op jit(solution)/shard_map/ppermute | solution.py:569
  74.9 22.1 %collective-permute-start.24 = (f32[2,256,128]{2,1,0:T(8,128)S(1)}, f32[2,256,128]{2,1,0:T(8,128)S(1)}, u32[]{:S(2)}, u32[]{:S(2)}) collective-permute-start(f32[2,256,128]{2,1,0:T(8,128)S(1)} %get-tuple-element.92), channel_id=1, source_target_pairs={{1,2},{2,1},{5,6},{6,5},{9,10},{10,9},{13,14},{14,13},{17,18},{18,... | collective-permute-start | bytes 786440 | tf_op jit(solution)/shard_map/ppermute | solution.py:574
  75.6 7.5 %collective-permute-start.14 = (f32[72,256]{1,0:T(8,128)S(1)}, f32[72,256]{1,0:T(8,128)S(1)}, u32[]{:S(2)}, u32[]{:S(2)}) collective-permute-start(f32[72,256]{1,0:T(8,128)S(1)} %add.4.refs_0_), channel_id=1, source_target_pairs={{0,2},{1,3},{2,0},{3,1},{4,6},{5,7},{6,4},{7,5},{8,10},{9,11},{10,... | collective-permute-start | bytes 221192 | tf_op jit(solution)/shard_map/ppermute | solution.py:569
  83.1 9.1 %collective-permute-start.17 = (f32[64,256]{1,0:T(8,128)S(1)}, f32[64,256]{1,0:T(8,128)S(1)}, u32[]{:S(2)}, u32[]{:S(2)}) collective-permute-start(f32[64,256]{1,0:T(8,128)S(1)} %slice.8.refs_0_), channel_id=1, source_target_pairs={{0,24},{4,28},{8,16},{12,20},{16,8},{20,12},{24,0},{28,4},{1,25},{... | collective-permute-start | bytes 196616 | tf_op jit(solution)/shard_map/ppermute | solution.py:569
  89.9 5.6 %collective-permute-start.16 = (f32[64,256]{1,0:T(8,128)S(1)}, f32[64,256]{1,0:T(8,128)S(1)}, u32[]{:S(2)}, u32[]{:S(2)}) collective-permute-start(f32[64,256]{1,0:T(8,128)S(1)} %slice.8.refs_0_), channel_id=1, source_target_pairs={{0,8},{4,12},{8,0},{12,4},{16,24},{20,28},{24,16},{28,20},{1,9},{5... | collective-permute-start | bytes 196616 | tf_op jit(solution)/shard_map/ppermute | solution.py:569
  89.9 6.9 %collective-permute-start.15 = (f32[64,256]{1,0:T(8,128)S(1)}, f32[64,256]{1,0:T(8,128)S(1)}, u32[]{:S(2)}, u32[]{:S(2)}) collective-permute-start(f32[64,256]{1,0:T(8,128)S(1)} %slice.8.refs_0_), channel_id=1, source_target_pairs={{0,16},{4,20},{8,24},{12,28},{16,0},{20,4},{24,8},{28,12},{1,17},{... | collective-permute-start | bytes 196616 | tf_op jit(solution)/shard_map/ppermute | solution.py:569
  (10 other events, 37.2 us)

commit v2 on v1

--- a/solution.py
+++ b/solution.py
@@ -179,9 +179,9 @@
                 ext[part, at, pl.ds(start, half), :] = strip[part, :, at * half : (at + 1) * half]
 
 
-def place(positions, slot_at, half):
-    row = positions[0, slot_at] + half
-    col = positions[1, slot_at] + half
+def place(places, slot_at, half):
+    row = places[0, slot_at] + half
+    col = places[1, slot_at] + half
     return row, col // half, col % half
 
 
@@ -238,7 +238,7 @@
     return high, middle, (rest - middle.astype(F32)).astype(BF16)
 
 
-def prepare_kernel(count, measured, propagator, matrices, targets, kernel_out, total):
+def prepare_kernel(places, measured, propagator, matrices, targets, kernel_out, level_scalars):
     slots = measured.shape[0]
 
     def reorder(source, at, out):
@@ -257,14 +257,19 @@
     for slot_at in range(slots):
         reorder(measured, slot_at, targets)
         sums = jnp.sum(measured[slot_at])
-        used = used + jnp.where(slot_at < count[0, 0], sums, jnp.float32(0.0))
+        used = used + jnp.where(slot_at < places[2, 0], sums, jnp.float32(0.0))
     for part in range(2):
         reorder(propagator, part, kernel_out)
-    total[0, 0] = used
+    width = level_scalars.shape[1]
+    level_scalars[...] = jnp.where(
+        lax.broadcasted_iota(jnp.int32, (SCALARS, width), 0) < SCALARS // 2,
+        jnp.full((SCALARS, width), used, F32),
+        jnp.full((SCALARS, width), places[2, 0].astype(F32), F32),
+    )
 
 
 def first_kernel(
-    count, positions, tiles, side_a, side_b, strip_a, strip_b, probe, transfer,
+    places, tiles, side_a, side_b, strip_a, strip_b, probe, transfer,
     turns, matrices,
     waves, patches, ext, work,
 ):
@@ -279,13 +284,13 @@
     first, second = matrices.at[0:2], matrices.at[2:4]
 
     def visit(pair_at, carry):
-        slots = [slot for slot, weight in pair_of(count[0, 0], pair_at)]
-        places = [place(positions, slot, half) for slot in slots]
+        slots = [slot for slot, weight in pair_of(places[2, 0], pair_at)]
+        spots = [place(places, slot, half) for slot in slots]
         works = [work.at[at] for at in range(2)]
         turn = lane_pair(turns)
         for at in chunks(width):
             rows = pl.ds(at, CHUNK)
-            for slot, (row, base, shift), field in zip(slots, places, works):
+            for slot, (row, base, shift), field in zip(slots, spots, works):
                 patch = tuple(
                     read_patch(ext, part, row + at, CHUNK, base, shift, half) for part in range(2)
                 )
@@ -304,11 +309,11 @@
                 waves[slot, 1, rows, :] = wave[1]
         return carry
 
-    lax.fori_loop(0, (count[0, 0] + 1) // 2, visit, 0)
+    lax.fori_loop(0, (places[2, 0] + 1) // 2, visit, 0)
 
 
 def second_kernel(
-    count, positions, tiles, side_a, side_b, strip_a, strip_b, waves, targets,
+    places, tiles, side_a, side_b, strip_a, strip_b, waves, targets,
     turns, matrices,
     backs, centre, send_a, send_b, ext, acc, patch, work,
 ):
@@ -320,9 +325,9 @@
     first, second = matrices.at[0:2], matrices.at[2:4]
 
     def visit(pair_at, carry):
-        pair = pair_of(count[0, 0], pair_at)
+        pair = pair_of(places[2, 0], pair_at)
         slots = [slot for slot, weight in pair]
-        places = [place(positions, slot, half) for slot in slots]
+        spots = [place(places, slot, half) for slot in slots]
         works = [work.at[at] for at in range(2)]
         turn = lane_pair(turns)
 
@@ -333,7 +338,7 @@
 
         for at in chunks(width):
             rows = pl.ds(at, CHUNK)
-            for which, (slot, (row, base, shift)) in enumerate(zip(slots, places)):
+            for which, (slot, (row, base, shift)) in enumerate(zip(slots, spots)):
                 cells = tuple(
                     read_patch(ext, part, row + at, CHUNK, base, shift, half) for part in range(2)
                 )
@@ -346,7 +351,7 @@
         left_stage(works, turns, first, second, [functools.partial(misfit, slot) for slot in slots])
         for at in chunks(width):
             rows = pl.ds(at, CHUNK)
-            for which, ((slot, weight), (row, base, shift)) in enumerate(zip(pair, places)):
+            for which, ((slot, weight), (row, base, shift)) in enumerate(zip(pair, spots)):
                 field = works[which]
                 adjoint = right_inverse((field[0, rows, :], field[1, rows, :]), turn, first)
                 wave = (waves[slot, 0, rows, :], waves[slot, 1, rows, :])
@@ -359,12 +364,12 @@
                 backs[slot, 1, rows, :] = out[1]
         return carry
 
-    lax.fori_loop(0, (count[0, 0] + 1) // 2, visit, 0)
+    lax.fori_loop(0, (places[2, 0] + 1) // 2, visit, 0)
     write_out(acc, device_bits(), centre, (send_a, send_b))
 
 
 def third_kernel(
-    count, positions, used, patches, backs, probe, transfer,
+    places, level_scalars, patches, backs, probe, transfer,
     turns, matrices,
     adjoints, keep, send, work, probe_sum,
 ):
@@ -379,7 +384,7 @@
     first, second = matrices.at[0:2], matrices.at[2:4]
 
     def visit(pair_at, carry):
-        pair = pair_of(count[0, 0], pair_at)
+        pair = pair_of(places[2, 0], pair_at)
         turn = lane_pair(turns)
         works = [work.at[at] for at in range(2)]
         for (slot, weight), own in zip(pair, works):
@@ -396,26 +401,22 @@
                     probe_sum[part, rows, :] = probe_sum[part, rows, :] + back[part] * weight
         return carry
 
-    lax.fori_loop(0, (count[0, 0] + 1) // 2, visit, 0)
+    lax.fori_loop(0, (places[2, 0] + 1) // 2, visit, 0)
     mine = device_bits()[0]
     keep[:width, :] = probe_sum[mine]
     send[:width, :] = probe_sum[1 - mine]
-    scalars = jnp.where(
-        lax.broadcasted_iota(jnp.int32, (SCALARS, width), 0) < SCALARS // 2,
-        jnp.full((SCALARS, width), used[0, 0], F32),
-        jnp.full((SCALARS, width), count[0, 0].astype(F32), F32),
-    )
+    scalars = level_scalars[...]
     keep[width:, :] = scalars
     send[width:, :] = scalars
 
 
-def fourth_kernel(count, positions, probe, adjoints, centre, send_a, send_b, acc):
+def fourth_kernel(places, probe, adjoints, centre, send_a, send_b, acc):
     width = probe.shape[1]
     half = width // 2
     acc[...] = jnp.zeros_like(acc)
 
     def visit(slot_at, carry):
-        row, base, shift = place(positions, slot_at, half)
+        row, base, shift = place(places, slot_at, half)
         for at in chunks(width):
             rows = pl.ds(at, CHUNK)
             adjoint = (adjoints[slot_at, 0, rows, :], adjoints[slot_at, 1, rows, :])
@@ -424,7 +425,7 @@
                 add_patch(acc, part, row + at, base, shift, term[part])
         return carry
 
-    lax.fori_loop(0, count[0, 0], visit, 0)
+    lax.fori_loop(0, places[2, 0], visit, 0)
     write_out(acc, device_bits(), centre, (send_a, send_b))
 
 
@@ -597,14 +598,14 @@
     side, strip, middle = (2, tile, half), (2, half, long), (2, tile, long)
     wide, one = (2, 3 + tile // half, long, half), (2, width, width)
     two = (2, *one)
-    places = positions[0, 0].T
+    places = jnp.concatenate([positions[0, 0].T, jnp.broadcast_to(scan_counts, (1, slots))], axis=0)
 
     edges = call(edges_kernel, [side] * (2 * layers), [], [], [object_slices], 0, "tile_edges")
     sides = [both_swaps(edges[2 * at : 2 * at + 2], "col") for at in range(layers)]
-    targets, transfer, used = call(
-        prepare_kernel, [(slots, width, width), one, (1, 1)], [], [scan_counts],
+    targets, transfer, level_scalars = call(
+        prepare_kernel, [(slots, width, width), one, (SCALARS, width)], [], [places],
         [measured[0, 0], propagator, matrices],
-        6, "reorder_targets", [VMEM, VMEM, SMEM],
+        6, "reorder_targets",
     )
     sides[0], targets, transfer = lax.optimization_barrier((sides[0], targets, transfer))
     strips = []
@@ -616,11 +617,11 @@
         strips.append(both_swaps(pair, "row"))
 
     waves, patches = call(
-        first_kernel, [fields, fields], [wide, two], [scan_counts, places],
+        first_kernel, [fields, fields], [wide, two], [places],
         [object_slices, *sides[0], *strips[0], probe, transfer, *transforms], 20, "first_slice",
     )
     backs, centre, *ends = call(
-        second_kernel, [fields, middle, strip, strip], [wide, wide, two, two], [scan_counts, places],
+        second_kernel, [fields, middle, strip, strip], [wide, wide, two, two], [places],
         [object_slices, *sides[1], *strips[1], waves, targets, *transforms], 20, "second_slice",
     )
 
@@ -639,28 +640,28 @@
     ends_last, centre_last = both_swaps(ends, "row"), centre
     message = (width + SCALARS, width)
     adjoints, keep, send = call(
-        third_kernel, [fields, message, message], [two, one], [scan_counts, places, used],
-        [patches, backs, probe, transfer, *transforms], 20, "first_adjoint",
-    )
-    keep, send = halve(2, keep, swap(send, "row", 1))
-    send, ends_last = lax.optimization_barrier((send, ends_last))
+        third_kernel, [fields, message, message], [two, one], [places],
+        [level_scalars, patches, backs, probe, transfer, *transforms], 20, "first_adjoint",
+    )
+    centre, *ends = call(
+        fourth_kernel, [middle, strip, strip], [wide], [places],
+        [probe, adjoints], 0, "first_gradient",
+    )
+    received, centre, ends = lax.optimization_barrier((swap(send, "row", 1), centre, ends))
+    keep, send = halve(2, keep, received)
+    send, ends, ends_last = lax.optimization_barrier((send, ends, ends_last))
+    ends = both_swaps(ends, "row")
     owned_last, *sides_last = add_rows(centre_last, ends_last)
     sides_last = both_swaps(sides_last, "col")
     keep, send = halve(3, keep, swap(send, "row", 2), 20)
-    send, adjoints = lax.optimization_barrier((send, adjoints))
-    centre, *ends = call(
-        fourth_kernel, [middle, strip, strip], [wide], [scan_counts, places],
-        [probe, adjoints], 20, "first_gradient",
-    )
-    ends = both_swaps(ends, "row")
-    (state,) = call(
-        add_kernel, [keep.shape], [], [], [keep, swap(send, "row", 4)], 20, "add",
-    )
-    ends, sides_last = lax.optimization_barrier((ends, sides_last))
+    state = keep + swap(send, "row", 4)
+    state, ends, sides_last = lax.optimization_barrier((state, ends, sides_last))
     owned_first, *sides_first = add_rows(centre, ends)
     sides_first = both_swaps(sides_first, "col")
-    (state,) = call(add_kernel, [state.shape], [], [], [state, swap(state, "col", 1)], 20, "add")
-    (state,) = call(add_kernel, [state.shape], [], [], [state, swap(state, "col", 2)], 0, "add")
+    (state,) = call(
+        add_kernel, [state.shape], [], [],
+        [state, *(swap(state, "col", bit) for bit in range(1, 4))], 20, "add",
+    )
     for axis, bit in (("col", 4), ("row", 8)):
         for bit in higher_bits(axis, bit):
             state = state + swap(state, axis, bit)

time: 99.5 us -> 96.4 us (0.969)
  starting transfers between devices: 47 us -> 41.9 us
    ppermute x17 -> x18, starting transfers between devices: 41.4 us -> 36.3 us  [swap(): lax.ppermute(value, axis, [(i, i ^ bit) for i in range(lax.axis_size(axis...]
    ppermute x17 -> x18, waiting for transfers between devices: 20.3 us -> 20.8 us  [swap(): lax.ppermute(value, axis, [(i, i ^ bit) for i in range(lax.axis_size(axis...]
    pallas_call x18 -> x16, Pallas kernels: 25.7 us -> 25.7 us  [call(): pl.pallas_call(kernel, out_shape=[jax.ShapeDtypeStruct(shape, F32) for sh...]
    unnamed x18 -> x16, local copies, waits for them, and re-layouts: 4.64 us -> 4.64 us
  transfers between devices with their start and end apart: 25 -> 26, of which waited for: 8 -> 7; matrix products, arithmetic and copies ran while one was open for 0% -> 1% of each run, Pallas kernels for 17% -> 18%
where the time goes in v2:
time: 96.4 us; the launch traced here: 95.5 us
  starting transfers between devices  41.9 us (43%)
  Pallas kernels  25.7 us (27%)
  waiting for transfers between devices  20.8 us (22%)
  local copies, waits for them, and re-layouts  5.34 us (6%)
  between operations  1.69 us (2%)
    ppermute x18, starting transfers between devices, swap(): lax.ppermute(value, axis, [(i, i ^ bit) for i in range(lax.axis_size(axis...  36.3 us
    pallas_call x16, Pallas kernels, call(): pl.pallas_call(kernel, out_shape=[jax.ShapeDtypeStruct(shape, F32) for sh...  25.7 us
    ppermute x18, waiting for transfers between devices, swap(): lax.ppermute(value, axis, [(i, i ^ bit) for i in range(lax.axis_size(axis...  20.8 us
    ppermute x8, starting transfers between devices, swap_next(): lax.ppermute(value, axis, [pair for i in odd for pair in ((i, i + 1), (i...  5.56 us
    unnamed x16, local copies, waits for them, and re-layouts  4.64 us
  transfers between devices with their start and end apart: 26, of which 7 were waited for; matrix products, arithmetic and copies ran while one was open for 1% of the time, Pallas kernels for 18%

profile of v2, /device:TPU:0, one launch (start us, length us, event | category | flops | bytes accessed | tf_op | source)
XLA Modules:
  0.0 95.5 jit_solution(5286836423132037903)
XLA Ops:
  0.6 1.2 %copy-done = f32[2,2,256,256]{3,2,1,0:T(8,128)S(1)} copy-done((f32[2,2,256,256]{3,2,1,0:T(8,128)S(1)}, f32[2,2,256,256]{3,2,1,0:T(8,128)}, u32[]{:S(2)}) %copy-start) | copy-done | bytes 1048600
  1.9 3.0 %collective-permute-start = (f32[2,256,128]{2,1,0:T(8,128)S(1)}, f32[2,256,128]{2,1,0:T(8,128)S(1)}, u32[]{:S(2)}, u32[]{:S(2)}) collective-permute-start(f32[2,256,128]{2,1,0:T(8,128)S(1)} %get-tuple-element.56), channel_id=1, source_target_pairs={{0,1},{1,0},{2,3},{3,2},{4,5},{5,4},{6,7},{7,6},{8,9},{9,8},{10,11... | collective-permute-start | bytes 786440 | tf_op jit(solution)/shard_map/ppermute | solution.py:570
  5.6 4.3 %collective-permute-start.4 = (f32[2,256,128]{2,1,0:T(8,128)S(1)}, f32[2,256,128]{2,1,0:T(8,128)S(1)}, u32[]{:S(2)}, u32[]{:S(2)}) collective-permute-start(f32[2,256,128]{2,1,0:T(8,128)S(1)} %get-tuple-element.66), channel_id=1, source_target_pairs={{0,1},{1,0},{2,3},{3,2},{4,5},{5,4},{6,7},{7,6},{8,9},{9,8},{10,11... | collective-permute-start | bytes 786440 | tf_op jit(solution)/shard_map/ppermute | solution.py:570
  11.9 1.2 %copy-done.3 = f32[1,1,4,256,256]{4,3,2,1,0:T(8,128)S(1)} copy-done((f32[1,1,4,256,256]{4,3,2,1,0:T(8,128)S(1)}, f32[1,1,4,256,256]{4,3,2,1,0:T(8,128)}, u32[]{:S(2)}) %copy-start.3) | copy-done | bytes 1048600
  13.1 1.0 %copy-done.4 = f32[2,256,256]{2,1,0:T(8,128)S(1)} copy-done((f32[2,256,256]{2,1,0:T(8,128)S(1)}, f32[2,256,256]{2,1,0:T(8,128)}, u32[]{:S(2)}) %copy-start.4) | copy-done | bytes 524312
  14.2 1.1 %copy-done.5 = bf16[6,256,256]{2,1,0:T(8,128)(2,1)S(1)} copy-done((bf16[6,256,256]{2,1,0:T(8,128)(2,1)S(1)}, bf16[6,256,256]{2,1,0:T(8,128)(2,1)}, u32[]{:S(2)}) %copy-start.5) | copy-done | bytes 786456
  15.3 2.3 %reorder_targets.1 = (f32[4,256,256]{2,1,0:T(8,128)S(1)}, f32[2,256,256]{2,1,0:T(8,128)S(1)}, f32[8,256]{1,0:T(8,128)S(1)}) custom-call(s32[3,4]{1,0:T(4,128)S(1)} %concatenate.3.places, f32[4,256,256]{2,1,0:T(8,128)S(1)} %bitcast.6, f32[2,256,256]{2,1,0:T(8,128)S(1)} %copy-done.4, bf16[6,256,256]{2,1,0:T(8,128)(2,1)S(1)} %copy-done.5), custom_call_target="tpu_custom_call" | custom-call | flops 6000000000 | bytes 3145728 | tf_op jit(solution)/shard_map/reorder_targets/pallas_call | solution.py:557
  18.7 4.6 %collective-permute-done.4.side_a = f32[2,256,128]{2,1,0:T(8,128)S(1)} collective-permute-done((f32[2,256,128]{2,1,0:T(8,128)S(1)}, f32[2,256,128]{2,1,0:T(8,128)S(1)}, u32[]{:S(2)}, u32[]{:S(2)}) %collective-permute-start.4) | collective-permute-done | bytes 262176 | tf_op jit(solution)/shard_map/ppermute | solution.py:570
  24.2 6.0 %first_slice.1 = (f32[4,2,256,256]{3,2,1,0:T(8,128)S(1)}, f32[4,2,256,256]{3,2,1,0:T(8,128)S(1)}) custom-call(s32[3,4]{1,0:T(4,128)S(1)} %concatenate.3.places, f32[2,2,256,256]{3,2,1,0:T(8,128)S(1)} %copy-done.1, f32[2,256,128]{2,1,0:T(8,128)S(1)} %collective-permute-done.side_a, f32[2,256,128]{2,1,0:T(8,128)S(1)} %collective-permute-done.1.side_b, ...), custom_call_target="tpu_custom_call" | custom-call | flops 20000000000 | bytes 5382144 | tf_op jit(solution)/shard_map/first_slice/pallas_call | solution.py:557
  30.3 7.9 %second_slice.1 = (f32[4,2,256,256]{3,2,1,0:T(8,128)S(1)}, f32[2,256,512]{2,1,0:T(8,128)S(1)}, f32[2,128,512]{2,1,0:T(8,128)S(1)}, f32[2,128,512]{2,1,0:T(8,128)S(1)}) custom-call(s32[3,4]{1,0:T(4,128)S(1)} %concatenate.3.places, f32[2,2,256,256]{3,2,1,0:T(8,128)S(1)} %copy-done.1, f32[2,256,128]{2,1,0:T(8,128)S(1)} %collective-permute-done.4.side_a, ...), custom_call_target="tpu_custom_call" | custom-call | flops 20000000000 | bytes 7479296 | tf_op jit(solution)/shard_map/second_slice/pallas_call | solution.py:557
  38.2 4.7 %collective-permute-start.9 = (f32[2,128,512]{2,1,0:T(8,128)S(1)}, f32[2,128,512]{2,1,0:T(8,128)S(1)}, u32[]{:S(2)}, u32[]{:S(2)}) collective-permute-start(f32[2,128,512]{2,1,0:T(8,128)S(1)} %get-tuple-element.84), channel_id=1, source_target_pairs={{0,4},{4,0},{8,12},{12,8},{16,20},{20,16},{24,28},{28,24},{1,5},{5... | collective-permute-start | bytes 1572872 | tf_op jit(solution)/shard_map/ppermute | solution.py:570
  43.7 4.8 %first_adjoint.1 = (f32[4,2,256,256]{3,2,1,0:T(8,128)S(1)}, f32[264,256]{1,0:T(8,128)S(1)}, f32[264,256]{1,0:T(8,128)S(1)}) custom-call(s32[3,4]{1,0:T(4,128)S(1)} %concatenate.3.places, f32[8,256]{1,0:T(8,128)S(1)} %get-tuple-element.55.level_scalars, f32[4,2,256,256]{3,2,1,0:T(8,128)S(1)} %get-tuple-element.65.patches, ...), custom_call_target="tpu_custom_call" | custom-call | flops 20000000000 | bytes 6963200 | tf_op jit(solution)/shard_map/first_adjoint/pallas_call | solution.py:557
  48.4 1.3 %collective-permute-start.8 = (f32[264,256]{1,0:T(8,128)S(1)}, f32[264,256]{1,0:T(8,128)S(1)}, u32[]{:S(2)}, u32[]{:S(2)}) collective-permute-start(f32[264,256]{1,0:T(8,128)S(1)} %get-tuple-element.74), channel_id=1, source_target_pairs={{0,4},{4,0},{8,12},{12,8},{16,20},{20,16},{24,28},{28,24},{1,5},{5... | collective-permute-start | bytes 811016 | tf_op jit(solution)/shard_map/ppermute | solution.py:570
  49.7 1.8 %first_gradient.1 = (f32[2,256,512]{2,1,0:T(8,128)S(1)}, f32[2,128,512]{2,1,0:T(8,128)S(1)}, f32[2,128,512]{2,1,0:T(8,128)S(1)}) custom-call(s32[3,4]{1,0:T(4,128)S(1)} %concatenate.3.places, f32[2,256,256]{2,1,0:T(8,128)S(1)} %copy-done.2, f32[4,2,256,256]{3,2,1,0:T(8,128)S(1)} %get-tuple-element.75.adjoints), custom_call_target="tpu_custom_call" | custom-call | bytes 2621440 | tf_op jit(solution)/shard_map/first_gradient/pallas_call | solution.py:557
  51.6 1.8 %collective-permute-start.11 = (f32[136,256]{1,0:T(8,128)S(1)}, f32[136,256]{1,0:T(8,128)S(1)}, u32[]{:S(2)}, u32[]{:S(2)}) collective-permute-start(f32[136,256]{1,0:T(8,128)S(1)} %get-tuple-element.86), channel_id=1, source_target_pairs={{0,8},{4,12},{8,0},{12,4},{16,24},{20,28},{24,16},{28,20},{1,9},{5... | collective-permute-start | bytes 417800 | tf_op jit(solution)/shard_map/ppermute | solution.py:570
  53.8 8.7 %collective-permute-start.15 = (f32[2,256,128]{2,1,0:T(8,128)S(1)}, f32[2,256,128]{2,1,0:T(8,128)S(1)}, u32[]{:S(2)}, u32[]{:S(2)}) collective-permute-start(f32[2,256,128]{2,1,0:T(8,128)S(1)} %get-tuple-element.94), channel_id=1, source_target_pairs={{0,1},{1,0},{2,3},{3,2},{4,5},{5,4},{6,7},{7,6},{8,9},{9,8},{10,11... | collective-permute-start | bytes 786440 | tf_op jit(solution)/shard_map/ppermute | solution.py:570
  64.0 2.8 %collective-permute-start.12 = (f32[72,256]{1,0:T(8,128)S(1)}, f32[72,256]{1,0:T(8,128)S(1)}, u32[]{:S(2)}, u32[]{:S(2)}) collective-permute-start(f32[72,256]{1,0:T(8,128)S(1)} %get-tuple-element.88), channel_id=1, source_target_pairs={{0,16},{4,20},{8,24},{12,28},{16,0},{20,4},{24,8},{28,12},{1,17},{... | collective-permute-start | bytes 221192 | tf_op jit(solution)/shard_map/ppermute | solution.py:570
  66.8 10.2 %collective-permute-done.12 = f32[72,256]{1,0:T(8,128)S(1)} collective-permute-done((f32[72,256]{1,0:T(8,128)S(1)}, f32[72,256]{1,0:T(8,128)S(1)}, u32[]{:S(2)}, u32[]{:S(2)}) %collective-permute-start.12) | collective-permute-done | bytes 73760 | tf_op jit(solution)/shard_map/ppermute | solution.py:570
  77.1 2.8 %collective-permute-start.18 = (f32[72,256]{1,0:T(8,128)S(1)}, f32[72,256]{1,0:T(8,128)S(1)}, u32[]{:S(2)}, u32[]{:S(2)}) collective-permute-start(f32[72,256]{1,0:T(8,128)S(1)} %add.6.refs_0_), channel_id=1, source_target_pairs={{0,2},{1,3},{2,0},{3,1},{4,6},{5,7},{6,4},{7,5},{8,10},{9,11},{10,... | collective-permute-start | bytes 221192 | tf_op jit(solution)/shard_map/ppermute | solution.py:570
  79.9 1.4 %collective-permute-start.17 = (f32[72,256]{1,0:T(8,128)S(1)}, f32[72,256]{1,0:T(8,128)S(1)}, u32[]{:S(2)}, u32[]{:S(2)}) collective-permute-start(f32[72,256]{1,0:T(8,128)S(1)} %add.6.refs_0_), channel_id=1, source_target_pairs={{0,1},{1,0},{2,3},{3,2},{4,5},{5,4},{6,7},{7,6},{8,9},{9,8},{10,11... | collective-permute-start | bytes 221192 | tf_op jit(solution)/shard_map/ppermute | solution.py:570
  83.0 3.0 %collective-permute-done.17.refs_1_ = f32[72,256]{1,0:T(8,128)S(1)} collective-permute-done((f32[72,256]{1,0:T(8,128)S(1)}, f32[72,256]{1,0:T(8,128)S(1)}, u32[]{:S(2)}, u32[]{:S(2)}) %collective-permute-start.17) | collective-permute-done | bytes 73760 | tf_op jit(solution)/shard_map/ppermute | solution.py:570
  86.6 3.9 %collective-permute-start.20 = (f32[64,256]{1,0:T(8,128)S(1)}, f32[64,256]{1,0:T(8,128)S(1)}, u32[]{:S(2)}, u32[]{:S(2)}) collective-permute-start(f32[64,256]{1,0:T(8,128)S(1)} %slice.8.refs_0_), channel_id=1, source_target_pairs={{0,16},{4,20},{8,24},{12,28},{16,0},{20,4},{24,8},{28,12},{1,17},{... | collective-permute-start | bytes 196616 | tf_op jit(solution)/shard_map/ppermute | solution.py:570
  90.5 1.8 %collective-permute-done.22.refs_3_ = f32[64,256]{1,0:T(8,128)S(1)} collective-permute-done((f32[64,256]{1,0:T(8,128)S(1)}, f32[64,256]{1,0:T(8,128)S(1)}, u32[]{:S(2)}, u32[]{:S(2)}) %collective-permute-start.22) | collective-permute-done | bytes 65568 | tf_op jit(solution)/shard_map/ppermute | solution.py:570
  93.1 1.1 %finish_object.1 = f32[2,2,256,256]{3,2,1,0:T(8,128)} custom-call(f32[8,256]{1,0:T(8,128)S(1)} %slice.9.scalars, f32[2,256,256]{2,1,0:T(8,128)S(1)} %get-tuple-element.100.refs_0_, f32[2,256,128]{2,1,0:T(8,128)S(1)} %collective-permute-done.24.refs_1_, f32[2,256,128]{2,1,0:T(8,128)S(1)} %collective-permute-done.25.refs_2_, ...), custom_call_target="tpu_custom_call" | custom-call | flops 20000000000 | bytes 2105344 | tf_op jit(solution)/shard_map/finish_object/pallas_call | solution.py:557
  (64 shorter events, 11.0 us)
Async XLA Ops:
  1.9 15.7 %collective-permute-start = (f32[2,256,128]{2,1,0:T(8,128)S(1)}, f32[2,256,128]{2,1,0:T(8,128)S(1)}, u32[]{:S(2)}, u32[]{:S(2)}) collective-permute-start(f32[2,256,128]{2,1,0:T(8,128)S(1)} %get-tuple-element.56), channel_id=1, source_target_pairs={{0,1},{1,0},{2,3},{3,2},{4,5},{5,4},{6,7},{7,6},{8,9},{9,8},{10,11... | collective-permute-start | bytes 786440 | tf_op jit(solution)/shard_map/ppermute | solution.py:570
  4.9 12.7 %collective-permute-start.1 = (f32[2,256,128]{2,1,0:T(8,128)S(1)}, f32[2,256,128]{2,1,0:T(8,128)S(1)}, u32[]{:S(2)}, u32[]{:S(2)}) collective-permute-start(f32[2,256,128]{2,1,0:T(8,128)S(1)} %get-tuple-element.57), channel_id=1, source_target_pairs={{1,2},{2,1},{5,6},{6,5},{9,10},{10,9},{13,14},{14,13},{17,18},{18,... | collective-permute-start | bytes 786440 | tf_op jit(solution)/shard_map/ppermute | solution.py:575
  5.6 17.7 %collective-permute-start.4 = (f32[2,256,128]{2,1,0:T(8,128)S(1)}, f32[2,256,128]{2,1,0:T(8,128)S(1)}, u32[]{:S(2)}, u32[]{:S(2)}) collective-permute-start(f32[2,256,128]{2,1,0:T(8,128)S(1)} %get-tuple-element.66), channel_id=1, source_target_pairs={{0,1},{1,0},{2,3},{3,2},{4,5},{5,4},{6,7},{7,6},{8,9},{9,8},{10,11... | collective-permute-start | bytes 786440 | tf_op jit(solution)/shard_map/ppermute | solution.py:570
  9.9 13.4 %collective-permute-start.5 = (f32[2,256,128]{2,1,0:T(8,128)S(1)}, f32[2,256,128]{2,1,0:T(8,128)S(1)}, u32[]{:S(2)}, u32[]{:S(2)}) collective-permute-start(f32[2,256,128]{2,1,0:T(8,128)S(1)} %get-tuple-element.67), channel_id=1, source_target_pairs={{1,2},{2,1},{5,6},{6,5},{9,10},{10,9},{13,14},{14,13},{17,18},{18,... | collective-permute-start | bytes 786440 | tf_op jit(solution)/shard_map/ppermute | solution.py:575
  17.7 6.4 %collective-permute-start.2 = (f32[2,128,512]{2,1,0:T(8,128)S(1)}, f32[2,128,512]{2,1,0:T(8,128)S(1)}, u32[]{:S(2)}, u32[]{:S(2)}) collective-permute-start(f32[2,128,512]{2,1,0:T(8,128)S(1)} %get-tuple-element.62), channel_id=1, source_target_pairs={{0,4},{4,0},{8,12},{12,8},{16,20},{20,16},{24,28},{28,24},{1,5},{5... | collective-permute-start | bytes 1572872 | tf_op jit(solution)/shard_map/ppermute | solution.py:570
  17.9 6.3 %collective-permute-start.3 = (f32[2,128,512]{2,1,0:T(8,128)S(1)}, f32[2,128,512]{2,1,0:T(8,128)S(1)}, u32[]{:S(2)}, u32[]{:S(2)}) collective-permute-start(f32[2,128,512]{2,1,0:T(8,128)S(1)} %get-tuple-element.63), channel_id=1, source_target_pairs={{4,8},{8,4},{12,16},{16,12},{20,24},{24,20},{5,9},{9,5},{13,17},{1... | collective-permute-start | bytes 1572872 | tf_op jit(solution)/shard_map/ppermute | solution.py:575
  23.4 6.9 %collective-permute-start.6 = (f32[2,128,512]{2,1,0:T(8,128)S(1)}, f32[2,128,512]{2,1,0:T(8,128)S(1)}, u32[]{:S(2)}, u32[]{:S(2)}) collective-permute-start(f32[2,128,512]{2,1,0:T(8,128)S(1)} %get-tuple-element.68), channel_id=1, source_target_pairs={{0,4},{4,0},{8,12},{12,8},{16,20},{20,16},{24,28},{28,24},{1,5},{5... | collective-permute-start | bytes 1572872 | tf_op jit(solution)/shard_map/ppermute | solution.py:570
  23.5 6.8 %collective-permute-start.7 = (f32[2,128,512]{2,1,0:T(8,128)S(1)}, f32[2,128,512]{2,1,0:T(8,128)S(1)}, u32[]{:S(2)}, u32[]{:S(2)}) collective-permute-start(f32[2,128,512]{2,1,0:T(8,128)S(1)} %get-tuple-element.69), channel_id=1, source_target_pairs={{4,8},{8,4},{12,16},{16,12},{20,24},{24,20},{5,9},{9,5},{13,17},{1... | collective-permute-start | bytes 1572872 | tf_op jit(solution)/shard_map/ppermute | solution.py:575
  38.2 13.3 %collective-permute-start.9 = (f32[2,128,512]{2,1,0:T(8,128)S(1)}, f32[2,128,512]{2,1,0:T(8,128)S(1)}, u32[]{:S(2)}, u32[]{:S(2)}) collective-permute-start(f32[2,128,512]{2,1,0:T(8,128)S(1)} %get-tuple-element.84), channel_id=1, source_target_pairs={{0,4},{4,0},{8,12},{12,8},{16,20},{20,16},{24,28},{28,24},{1,5},{5... | collective-permute-start | bytes 1572872 | tf_op jit(solution)/shard_map/ppermute | solution.py:570
  43.0 8.6 %collective-permute-start.10 = (f32[2,128,512]{2,1,0:T(8,128)S(1)}, f32[2,128,512]{2,1,0:T(8,128)S(1)}, u32[]{:S(2)}, u32[]{:S(2)}) collective-permute-start(f32[2,128,512]{2,1,0:T(8,128)S(1)} %get-tuple-element.85), channel_id=1, source_target_pairs={{4,8},{8,4},{12,16},{16,12},{20,24},{24,20},{5,9},{9,5},{13,17},{1... | collective-permute-start | bytes 1572872 | tf_op jit(solution)/shard_map/ppermute | solution.py:575
  51.6 12.3 %collective-permute-start.11 = (f32[136,256]{1,0:T(8,128)S(1)}, f32[136,256]{1,0:T(8,128)S(1)}, u32[]{:S(2)}, u32[]{:S(2)}) collective-permute-start(f32[136,256]{1,0:T(8,128)S(1)} %get-tuple-element.86), channel_id=1, source_target_pairs={{0,8},{4,12},{8,0},{12,4},{16,24},{20,28},{24,16},{28,20},{1,9},{5... | collective-permute-start | bytes 417800 | tf_op jit(solution)/shard_map/ppermute | solution.py:570
  53.8 23.2 %collective-permute-start.15 = (f32[2,256,128]{2,1,0:T(8,128)S(1)}, f32[2,256,128]{2,1,0:T(8,128)S(1)}, u32[]{:S(2)}, u32[]{:S(2)}) collective-permute-start(f32[2,256,128]{2,1,0:T(8,128)S(1)} %get-tuple-element.94), channel_id=1, source_target_pairs={{0,1},{1,0},{2,3},{3,2},{4,5},{5,4},{6,7},{7,6},{8,9},{9,8},{10,11... | collective-permute-start | bytes 786440 | tf_op jit(solution)/shard_map/ppermute | solution.py:570
  62.5 14.5 %collective-permute-start.16 = (f32[2,256,128]{2,1,0:T(8,128)S(1)}, f32[2,256,128]{2,1,0:T(8,128)S(1)}, u32[]{:S(2)}, u32[]{:S(2)}) collective-permute-start(f32[2,256,128]{2,1,0:T(8,128)S(1)} %get-tuple-element.95), channel_id=1, source_target_pairs={{1,2},{2,1},{5,6},{6,5},{9,10},{10,9},{13,14},{14,13},{17,18},{18,... | collective-permute-start | bytes 786440 | tf_op jit(solution)/shard_map/ppermute | solution.py:575
  63.1 13.9 %collective-permute-start.13 = (f32[2,128,512]{2,1,0:T(8,128)S(1)}, f32[2,128,512]{2,1,0:T(8,128)S(1)}, u32[]{:S(2)}, u32[]{:S(2)}) collective-permute-start(f32[2,128,512]{2,1,0:T(8,128)S(1)} %get-tuple-element.89), channel_id=1, source_target_pairs={{0,4},{4,0},{8,12},{12,8},{16,20},{20,16},{24,28},{28,24},{1,5},{5... | collective-permute-start | bytes 1572872 | tf_op jit(solution)/shard_map/ppermute | solution.py:570
  63.2 13.8 %collective-permute-start.14 = (f32[2,128,512]{2,1,0:T(8,128)S(1)}, f32[2,128,512]{2,1,0:T(8,128)S(1)}, u32[]{:S(2)}, u32[]{:S(2)}) collective-permute-start(f32[2,128,512]{2,1,0:T(8,128)S(1)} %get-tuple-element.90), channel_id=1, source_target_pairs={{4,8},{8,4},{12,16},{16,12},{20,24},{24,20},{5,9},{9,5},{13,17},{1... | collective-permute-start | bytes 1572872 | tf_op jit(solution)/shard_map/ppermute | solution.py:575
  64.0 13.0 %collective-permute-start.12 = (f32[72,256]{1,0:T(8,128)S(1)}, f32[72,256]{1,0:T(8,128)S(1)}, u32[]{:S(2)}, u32[]{:S(2)}) collective-permute-start(f32[72,256]{1,0:T(8,128)S(1)} %get-tuple-element.88), channel_id=1, source_target_pairs={{0,16},{4,20},{8,24},{12,28},{16,0},{20,4},{24,8},{28,12},{1,17},{... | collective-permute-start | bytes 221192 | tf_op jit(solution)/shard_map/ppermute | solution.py:570
  77.0 5.8 %collective-permute-start.19 = (f32[72,256]{1,0:T(8,128)S(1)}, f32[72,256]{1,0:T(8,128)S(1)}, u32[]{:S(2)}, u32[]{:S(2)}) collective-permute-start(f32[72,256]{1,0:T(8,128)S(1)} %add.6.refs_0_), channel_id=1, source_target_pairs={{0,3},{1,2},{2,1},{3,0},{4,7},{5,6},{6,5},{7,4},{8,11},{9,10},{10,... | collective-permute-start | bytes 221192 | tf_op jit(solution)/shard_map/ppermute | solution.py:570
  77.1 5.9 %collective-permute-start.18 = (f32[72,256]{1,0:T(8,128)S(1)}, f32[72,256]{1,0:T(8,128)S(1)}, u32[]{:S(2)}, u32[]{:S(2)}) collective-permute-start(f32[72,256]{1,0:T(8,128)S(1)} %add.6.refs_0_), channel_id=1, source_target_pairs={{0,2},{1,3},{2,0},{3,1},{4,6},{5,7},{6,4},{7,5},{8,10},{9,11},{10,... | collective-permute-start | bytes 221192 | tf_op jit(solution)/shard_map/ppermute | solution.py:570
  79.9 6.1 %collective-permute-start.17 = (f32[72,256]{1,0:T(8,128)S(1)}, f32[72,256]{1,0:T(8,128)S(1)}, u32[]{:S(2)}, u32[]{:S(2)}) collective-permute-start(f32[72,256]{1,0:T(8,128)S(1)} %add.6.refs_0_), channel_id=1, source_target_pairs={{0,1},{1,0},{2,3},{3,2},{4,5},{5,4},{6,7},{7,6},{8,9},{9,8},{10,11... | collective-permute-start | bytes 221192 | tf_op jit(solution)/shard_map/ppermute | solution.py:570
  81.5 11.6 %collective-permute-start.24 = (f32[2,256,128]{2,1,0:T(8,128)S(1)}, f32[2,256,128]{2,1,0:T(8,128)S(1)}, u32[]{:S(2)}, u32[]{:S(2)}) collective-permute-start(f32[2,256,128]{2,1,0:T(8,128)S(1)} %get-tuple-element.101), channel_id=1, source_target_pairs={{0,1},{1,0},{2,3},{3,2},{4,5},{5,4},{6,7},{7,6},{8,9},{9,8},{10,11... | collective-permute-start | bytes 786440 | tf_op jit(solution)/shard_map/ppermute | solution.py:570
  82.2 10.9 %collective-permute-start.25 = (f32[2,256,128]{2,1,0:T(8,128)S(1)}, f32[2,256,128]{2,1,0:T(8,128)S(1)}, u32[]{:S(2)}, u32[]{:S(2)}) collective-permute-start(f32[2,256,128]{2,1,0:T(8,128)S(1)} %get-tuple-element.102), channel_id=1, source_target_pairs={{1,2},{2,1},{5,6},{6,5},{9,10},{10,9},{13,14},{14,13},{17,18},{18,... | collective-permute-start | bytes 786440 | tf_op jit(solution)/shard_map/ppermute | solution.py:575
  86.1 6.2 %collective-permute-start.22 = (f32[64,256]{1,0:T(8,128)S(1)}, f32[64,256]{1,0:T(8,128)S(1)}, u32[]{:S(2)}, u32[]{:S(2)}) collective-permute-start(f32[64,256]{1,0:T(8,128)S(1)} %slice.8.refs_0_), channel_id=1, source_target_pairs={{0,24},{4,28},{8,16},{12,20},{16,8},{20,12},{24,0},{28,4},{1,25},{... | collective-permute-start | bytes 196616 | tf_op jit(solution)/shard_map/ppermute | solution.py:570
  86.1 6.2 %collective-permute-start.21 = (f32[64,256]{1,0:T(8,128)S(1)}, f32[64,256]{1,0:T(8,128)S(1)}, u32[]{:S(2)}, u32[]{:S(2)}) collective-permute-start(f32[64,256]{1,0:T(8,128)S(1)} %slice.8.refs_0_), channel_id=1, source_target_pairs={{0,8},{4,12},{8,0},{12,4},{16,24},{20,28},{24,16},{28,20},{1,9},{5... | collective-permute-start | bytes 196616 | tf_op jit(solution)/shard_map/ppermute | solution.py:570
  86.6 6.3 %collective-permute-start.20 = (f32[64,256]{1,0:T(8,128)S(1)}, f32[64,256]{1,0:T(8,128)S(1)}, u32[]{:S(2)}, u32[]{:S(2)}) collective-permute-start(f32[64,256]{1,0:T(8,128)S(1)} %slice.8.refs_0_), channel_id=1, source_target_pairs={{0,16},{4,20},{8,24},{12,28},{16,0},{20,4},{24,8},{28,12},{1,17},{... | collective-permute-start | bytes 196616 | tf_op jit(solution)/shard_map/ppermute | solution.py:570
  (10 other events, 30.8 us)

commit v3 on v2

--- a/solution.py
+++ b/solution.py
@@ -269,7 +269,7 @@
 
 
 def first_kernel(
-    places, tiles, side_a, side_b, strip_a, strip_b, probe, transfer,
+    places, tiles, side_a, side_b, strip_b, strip_a, probe, transfer,
     turns, matrices,
     waves, patches, ext, work,
 ):
@@ -313,7 +313,7 @@
 
 
 def second_kernel(
-    places, tiles, side_a, side_b, strip_a, strip_b, waves, targets,
+    places, tiles, side_a, side_b, strip_b, strip_a, waves, targets,
     turns, matrices,
     backs, centre, send_a, send_b, ext, acc, patch, work,
 ):
@@ -459,7 +459,7 @@
         work(0, 1)
 
 
-def rows_kernel(centre, strip_a, strip_b, owned, side_a, side_b):
+def rows_kernel(centre, strip_b, strip_a, owned, side_a, side_b):
     bits = device_bits()
     half = strip_a.shape[1]
     size = centre.shape[1]
@@ -576,6 +576,9 @@
 
 
 def both_swaps(values, axis):
+    if axis == "row":
+        later = swap_next(values[1], axis)
+        return [later, swap(values[0], axis, 1)]
     return [swap(values[0], axis, 1), swap_next(values[1], axis)]
 
 

time: 96.4 us -> 96.9 us (level)
  starting transfers between devices: 41.9 us -> 54.1 us
  Pallas kernels: 25.7 us -> 17 us
  waiting for transfers between devices: 20.8 us -> 18.4 us
    ppermute x18, starting transfers between devices: 36.3 us -> 48.6 us  [swap(): lax.ppermute(value, axis, [(i, i ^ bit) for i in range(lax.axis_size(axis...]
    pallas_call x16, Pallas kernels: 25.7 us -> 17 us  [call(): pl.pallas_call(kernel, out_shape=[jax.ShapeDtypeStruct(shape, F32) for sh...]
    ppermute x18, waiting for transfers between devices: 20.8 us -> 18.4 us  [swap(): lax.ppermute(value, axis, [(i, i ^ bit) for i in range(lax.axis_size(axis...]
  transfers between devices with their start and end apart: 26 -> 26, of which waited for: 7 -> 8; matrix products, arithmetic and copies ran while one was open for 1% -> 1% of each run, Pallas kernels for 18% -> 12%
where the time goes in v3:
time: 96.9 us; the launch traced here: 96.5 us
  starting transfers between devices  54.1 us (56%)
  waiting for transfers between devices  18.4 us (19%)
  Pallas kernels  17 us (18%)
  local copies, waits for them, and re-layouts  5.34 us (6%)
  between operations  1.63 us (2%)
    ppermute x18, starting transfers between devices, swap(): lax.ppermute(value, axis, [(i, i ^ bit) for i in range(lax.axis_size(axis...  48.6 us
    ppermute x18, waiting for transfers between devices, swap(): lax.ppermute(value, axis, [(i, i ^ bit) for i in range(lax.axis_size(axis...  18.4 us
    pallas_call x16, Pallas kernels, call(): pl.pallas_call(kernel, out_shape=[jax.ShapeDtypeStruct(shape, F32) for sh...  17 us
    ppermute x8, starting transfers between devices, swap_next(): lax.ppermute(value, axis, [pair for i in odd for pair in ((i, i + 1), (i...  5.44 us
    unnamed x16, local copies, waits for them, and re-layouts  4.64 us
  transfers between devices with their start and end apart: 26, of which 8 were waited for; matrix products, arithmetic and copies ran while one was open for 1% of the time, Pallas kernels for 12%

profile of v3, /device:TPU:0, one launch (start us, length us, event | category | flops | bytes accessed | tf_op | source)
XLA Modules:
  0.0 96.5 jit_solution(16903654067516663847)
XLA Ops:
  0.6 1.2 %copy-done = f32[2,2,256,256]{3,2,1,0:T(8,128)S(1)} copy-done((f32[2,2,256,256]{3,2,1,0:T(8,128)S(1)}, f32[2,2,256,256]{3,2,1,0:T(8,128)}, u32[]{:S(2)}) %copy-start) | copy-done | bytes 1048600
  1.9 3.0 %collective-permute-start = (f32[2,256,128]{2,1,0:T(8,128)S(1)}, f32[2,256,128]{2,1,0:T(8,128)S(1)}, u32[]{:S(2)}, u32[]{:S(2)}) collective-permute-start(f32[2,256,128]{2,1,0:T(8,128)S(1)} %get-tuple-element.56), channel_id=1, source_target_pairs={{0,1},{1,0},{2,3},{3,2},{4,5},{5,4},{6,7},{7,6},{8,9},{9,8},{10,11... | collective-permute-start | bytes 786440 | tf_op jit(solution)/shard_map/ppermute | solution.py:570
  5.6 4.3 %collective-permute-start.4 = (f32[2,256,128]{2,1,0:T(8,128)S(1)}, f32[2,256,128]{2,1,0:T(8,128)S(1)}, u32[]{:S(2)}, u32[]{:S(2)}) collective-permute-start(f32[2,256,128]{2,1,0:T(8,128)S(1)} %get-tuple-element.66), channel_id=1, source_target_pairs={{0,1},{1,0},{2,3},{3,2},{4,5},{5,4},{6,7},{7,6},{8,9},{9,8},{10,11... | collective-permute-start | bytes 786440 | tf_op jit(solution)/shard_map/ppermute | solution.py:570
  11.9 1.2 %copy-done.3 = f32[1,1,4,256,256]{4,3,2,1,0:T(8,128)S(1)} copy-done((f32[1,1,4,256,256]{4,3,2,1,0:T(8,128)S(1)}, f32[1,1,4,256,256]{4,3,2,1,0:T(8,128)}, u32[]{:S(2)}) %copy-start.3) | copy-done | bytes 1048600
  14.2 1.1 %copy-done.5 = bf16[6,256,256]{2,1,0:T(8,128)(2,1)S(1)} copy-done((bf16[6,256,256]{2,1,0:T(8,128)(2,1)S(1)}, bf16[6,256,256]{2,1,0:T(8,128)(2,1)}, u32[]{:S(2)}) %copy-start.5) | copy-done | bytes 786456
  15.3 2.3 %reorder_targets.1 = (f32[4,256,256]{2,1,0:T(8,128)S(1)}, f32[2,256,256]{2,1,0:T(8,128)S(1)}, f32[8,256]{1,0:T(8,128)S(1)}) custom-call(s32[3,4]{1,0:T(4,128)S(1)} %concatenate.3.places, f32[4,256,256]{2,1,0:T(8,128)S(1)} %bitcast.6, f32[2,256,256]{2,1,0:T(8,128)S(1)} %copy-done.4, bf16[6,256,256]{2,1,0:T(8,128)(2,1)S(1)} %copy-done.5), custom_call_target="tpu_custom_call" | custom-call | flops 6000000000 | bytes 3145728 | tf_op jit(solution)/shard_map/reorder_targets/pallas_call | solution.py:557
  18.4 3.0 %collective-permute-start.3 = (f32[2,128,512]{2,1,0:T(8,128)S(1)}, f32[2,128,512]{2,1,0:T(8,128)S(1)}, u32[]{:S(2)}, u32[]{:S(2)}) collective-permute-start(f32[2,128,512]{2,1,0:T(8,128)S(1)} %get-tuple-element.63), channel_id=1, source_target_pairs={{0,4},{4,0},{8,12},{12,8},{16,20},{20,16},{24,28},{28,24},{1,5},{5... | collective-permute-start | bytes 1572872 | tf_op jit(solution)/shard_map/ppermute | solution.py:570
  21.4 1.9 %collective-permute-done.4.side_a = f32[2,256,128]{2,1,0:T(8,128)S(1)} collective-permute-done((f32[2,256,128]{2,1,0:T(8,128)S(1)}, f32[2,256,128]{2,1,0:T(8,128)S(1)}, u32[]{:S(2)}, u32[]{:S(2)}) %collective-permute-start.4) | collective-permute-done | bytes 262176 | tf_op jit(solution)/shard_map/ppermute | solution.py:570
  24.1 3.5 %collective-permute-start.7 = (f32[2,128,512]{2,1,0:T(8,128)S(1)}, f32[2,128,512]{2,1,0:T(8,128)S(1)}, u32[]{:S(2)}, u32[]{:S(2)}) collective-permute-start(f32[2,128,512]{2,1,0:T(8,128)S(1)} %get-tuple-element.69), channel_id=1, source_target_pairs={{0,4},{4,0},{8,12},{12,8},{16,20},{20,16},{24,28},{28,24},{1,5},{5... | collective-permute-start | bytes 1572872 | tf_op jit(solution)/shard_map/ppermute | solution.py:570
  27.7 3.3 %first_slice.1 = (f32[4,2,256,256]{3,2,1,0:T(8,128)S(1)}, f32[4,2,256,256]{3,2,1,0:T(8,128)S(1)}) custom-call(s32[3,4]{1,0:T(4,128)S(1)} %concatenate.3.places, f32[2,2,256,256]{3,2,1,0:T(8,128)S(1)} %copy-done.1, f32[2,256,128]{2,1,0:T(8,128)S(1)} %collective-permute-done.side_a, f32[2,256,128]{2,1,0:T(8,128)S(1)} %collective-permute-done.1.side_b, ...), custom_call_target="tpu_custom_call" | custom-call | flops 20000000000 | bytes 5382144 | tf_op jit(solution)/shard_map/first_slice/pallas_call | solution.py:557
  31.1 4.5 %second_slice.1 = (f32[4,2,256,256]{3,2,1,0:T(8,128)S(1)}, f32[2,256,512]{2,1,0:T(8,128)S(1)}, f32[2,128,512]{2,1,0:T(8,128)S(1)}, f32[2,128,512]{2,1,0:T(8,128)S(1)}) custom-call(s32[3,4]{1,0:T(4,128)S(1)} %concatenate.3.places, f32[2,2,256,256]{3,2,1,0:T(8,128)S(1)} %copy-done.1, f32[2,256,128]{2,1,0:T(8,128)S(1)} %collective-permute-done.4.side_a, ...), custom_call_target="tpu_custom_call" | custom-call | flops 20000000000 | bytes 7479296 | tf_op jit(solution)/shard_map/second_slice/pallas_call | solution.py:557
  36.3 6.4 %collective-permute-start.10 = (f32[2,128,512]{2,1,0:T(8,128)S(1)}, f32[2,128,512]{2,1,0:T(8,128)S(1)}, u32[]{:S(2)}, u32[]{:S(2)}) collective-permute-start(f32[2,128,512]{2,1,0:T(8,128)S(1)} %get-tuple-element.85), channel_id=1, source_target_pairs={{0,4},{4,0},{8,12},{12,8},{16,20},{20,16},{24,28},{28,24},{1,5},{5... | collective-permute-start | bytes 1572872 | tf_op jit(solution)/shard_map/ppermute | solution.py:570
  42.7 2.7 %first_adjoint.1 = (f32[4,2,256,256]{3,2,1,0:T(8,128)S(1)}, f32[264,256]{1,0:T(8,128)S(1)}, f32[264,256]{1,0:T(8,128)S(1)}) custom-call(s32[3,4]{1,0:T(4,128)S(1)} %concatenate.3.places, f32[8,256]{1,0:T(8,128)S(1)} %get-tuple-element.55.level_scalars, f32[4,2,256,256]{3,2,1,0:T(8,128)S(1)} %get-tuple-element.65.patches, ...), custom_call_target="tpu_custom_call" | custom-call | flops 20000000000 | bytes 6963200 | tf_op jit(solution)/shard_map/first_adjoint/pallas_call | solution.py:557
  45.4 1.3 %first_gradient.1 = (f32[2,256,512]{2,1,0:T(8,128)S(1)}, f32[2,128,512]{2,1,0:T(8,128)S(1)}, f32[2,128,512]{2,1,0:T(8,128)S(1)}) custom-call(s32[3,4]{1,0:T(4,128)S(1)} %concatenate.3.places, f32[2,256,256]{2,1,0:T(8,128)S(1)} %copy-done.2, f32[4,2,256,256]{3,2,1,0:T(8,128)S(1)} %get-tuple-element.75.adjoints), custom_call_target="tpu_custom_call" | custom-call | bytes 2621440 | tf_op jit(solution)/shard_map/first_gradient/pallas_call | solution.py:557
  47.0 4.0 %collective-permute-start.11 = (f32[136,256]{1,0:T(8,128)S(1)}, f32[136,256]{1,0:T(8,128)S(1)}, u32[]{:S(2)}, u32[]{:S(2)}) collective-permute-start(f32[136,256]{1,0:T(8,128)S(1)} %get-tuple-element.86), channel_id=1, source_target_pairs={{0,8},{4,12},{8,0},{12,4},{16,24},{20,28},{24,16},{28,20},{1,9},{5... | collective-permute-start | bytes 417800 | tf_op jit(solution)/shard_map/ppermute | solution.py:570
  51.5 8.2 %collective-permute-start.15 = (f32[2,256,128]{2,1,0:T(8,128)S(1)}, f32[2,256,128]{2,1,0:T(8,128)S(1)}, u32[]{:S(2)}, u32[]{:S(2)}) collective-permute-start(f32[2,256,128]{2,1,0:T(8,128)S(1)} %get-tuple-element.94), channel_id=1, source_target_pairs={{0,1},{1,0},{2,3},{3,2},{4,5},{5,4},{6,7},{7,6},{8,9},{9,8},{10,11... | collective-permute-start | bytes 786440 | tf_op jit(solution)/shard_map/ppermute | solution.py:570
  61.1 3.0 %collective-permute-start.14 = (f32[2,128,512]{2,1,0:T(8,128)S(1)}, f32[2,128,512]{2,1,0:T(8,128)S(1)}, u32[]{:S(2)}, u32[]{:S(2)}) collective-permute-start(f32[2,128,512]{2,1,0:T(8,128)S(1)} %get-tuple-element.90), channel_id=1, source_target_pairs={{0,4},{4,0},{8,12},{12,8},{16,20},{20,16},{24,28},{28,24},{1,5},{5... | collective-permute-start | bytes 1572872 | tf_op jit(solution)/shard_map/ppermute | solution.py:570
  64.1 3.3 %collective-permute-start.12 = (f32[72,256]{1,0:T(8,128)S(1)}, f32[72,256]{1,0:T(8,128)S(1)}, u32[]{:S(2)}, u32[]{:S(2)}) collective-permute-start(f32[72,256]{1,0:T(8,128)S(1)} %get-tuple-element.88), channel_id=1, source_target_pairs={{0,16},{4,20},{8,24},{12,28},{16,0},{20,4},{24,8},{28,12},{1,17},{... | collective-permute-start | bytes 221192 | tf_op jit(solution)/shard_map/ppermute | solution.py:570
  67.3 10.0 %collective-permute-done.12 = f32[72,256]{1,0:T(8,128)S(1)} collective-permute-done((f32[72,256]{1,0:T(8,128)S(1)}, f32[72,256]{1,0:T(8,128)S(1)}, u32[]{:S(2)}, u32[]{:S(2)}) %collective-permute-start.12) | collective-permute-done | bytes 73760 | tf_op jit(solution)/shard_map/ppermute | solution.py:570
  78.0 2.7 %collective-permute-start.18 = (f32[72,256]{1,0:T(8,128)S(1)}, f32[72,256]{1,0:T(8,128)S(1)}, u32[]{:S(2)}, u32[]{:S(2)}) collective-permute-start(f32[72,256]{1,0:T(8,128)S(1)} %add.6.refs_0_), channel_id=1, source_target_pairs={{0,2},{1,3},{2,0},{3,1},{4,6},{5,7},{6,4},{7,5},{8,10},{9,11},{10,... | collective-permute-start | bytes 221192 | tf_op jit(solution)/shard_map/ppermute | solution.py:570
  83.6 1.2 %collective-permute-done.18.refs_2_ = f32[72,256]{1,0:T(8,128)S(1)} collective-permute-done((f32[72,256]{1,0:T(8,128)S(1)}, f32[72,256]{1,0:T(8,128)S(1)}, u32[]{:S(2)}, u32[]{:S(2)}) %collective-permute-start.18) | collective-permute-done | bytes 73760 | tf_op jit(solution)/shard_map/ppermute | solution.py:570
  84.9 1.6 %collective-permute-done.17.refs_1_ = f32[72,256]{1,0:T(8,128)S(1)} collective-permute-done((f32[72,256]{1,0:T(8,128)S(1)}, f32[72,256]{1,0:T(8,128)S(1)}, u32[]{:S(2)}, u32[]{:S(2)}) %collective-permute-start.17) | collective-permute-done | bytes 73760 | tf_op jit(solution)/shard_map/ppermute | solution.py:570
  87.6 3.3 %collective-permute-start.20 = (f32[64,256]{1,0:T(8,128)S(1)}, f32[64,256]{1,0:T(8,128)S(1)}, u32[]{:S(2)}, u32[]{:S(2)}) collective-permute-start(f32[64,256]{1,0:T(8,128)S(1)} %slice.8.refs_0_), channel_id=1, source_target_pairs={{0,16},{4,20},{8,24},{12,28},{16,0},{20,4},{24,8},{28,12},{1,17},{... | collective-permute-start | bytes 196616 | tf_op jit(solution)/shard_map/ppermute | solution.py:570
  90.9 2.2 %collective-permute-done.22.refs_3_ = f32[64,256]{1,0:T(8,128)S(1)} collective-permute-done((f32[64,256]{1,0:T(8,128)S(1)}, f32[64,256]{1,0:T(8,128)S(1)}, u32[]{:S(2)}, u32[]{:S(2)}) %collective-permute-start.22) | collective-permute-done | bytes 65568 | tf_op jit(solution)/shard_map/ppermute | solution.py:570
  (64 shorter events, 15.6 us)
Async XLA Ops:
  1.9 15.6 %collective-permute-start = (f32[2,256,128]{2,1,0:T(8,128)S(1)}, f32[2,256,128]{2,1,0:T(8,128)S(1)}, u32[]{:S(2)}, u32[]{:S(2)}) collective-permute-start(f32[2,256,128]{2,1,0:T(8,128)S(1)} %get-tuple-element.56), channel_id=1, source_target_pairs={{0,1},{1,0},{2,3},{3,2},{4,5},{5,4},{6,7},{7,6},{8,9},{9,8},{10,11... | collective-permute-start | bytes 786440 | tf_op jit(solution)/shard_map/ppermute | solution.py:570
  4.9 12.6 %collective-permute-start.1 = (f32[2,256,128]{2,1,0:T(8,128)S(1)}, f32[2,256,128]{2,1,0:T(8,128)S(1)}, u32[]{:S(2)}, u32[]{:S(2)}) collective-permute-start(f32[2,256,128]{2,1,0:T(8,128)S(1)} %get-tuple-element.57), channel_id=1, source_target_pairs={{1,2},{2,1},{5,6},{6,5},{9,10},{10,9},{13,14},{14,13},{17,18},{18,... | collective-permute-start | bytes 786440 | tf_op jit(solution)/shard_map/ppermute | solution.py:575
  5.6 17.7 %collective-permute-start.4 = (f32[2,256,128]{2,1,0:T(8,128)S(1)}, f32[2,256,128]{2,1,0:T(8,128)S(1)}, u32[]{:S(2)}, u32[]{:S(2)}) collective-permute-start(f32[2,256,128]{2,1,0:T(8,128)S(1)} %get-tuple-element.66), channel_id=1, source_target_pairs={{0,1},{1,0},{2,3},{3,2},{4,5},{5,4},{6,7},{7,6},{8,9},{9,8},{10,11... | collective-permute-start | bytes 786440 | tf_op jit(solution)/shard_map/ppermute | solution.py:570
  9.9 13.4 %collective-permute-start.5 = (f32[2,256,128]{2,1,0:T(8,128)S(1)}, f32[2,256,128]{2,1,0:T(8,128)S(1)}, u32[]{:S(2)}, u32[]{:S(2)}) collective-permute-start(f32[2,256,128]{2,1,0:T(8,128)S(1)} %get-tuple-element.67), channel_id=1, source_target_pairs={{1,2},{2,1},{5,6},{6,5},{9,10},{10,9},{13,14},{14,13},{17,18},{18,... | collective-permute-start | bytes 786440 | tf_op jit(solution)/shard_map/ppermute | solution.py:575
  17.7 10.0 %collective-permute-start.2 = (f32[2,128,512]{2,1,0:T(8,128)S(1)}, f32[2,128,512]{2,1,0:T(8,128)S(1)}, u32[]{:S(2)}, u32[]{:S(2)}) collective-permute-start(f32[2,128,512]{2,1,0:T(8,128)S(1)} %get-tuple-element.62), channel_id=1, source_target_pairs={{4,8},{8,4},{12,16},{16,12},{20,24},{24,20},{5,9},{9,5},{13,17},{1... | collective-permute-start | bytes 1572872 | tf_op jit(solution)/shard_map/ppermute | solution.py:575
  18.4 9.2 %collective-permute-start.3 = (f32[2,128,512]{2,1,0:T(8,128)S(1)}, f32[2,128,512]{2,1,0:T(8,128)S(1)}, u32[]{:S(2)}, u32[]{:S(2)}) collective-permute-start(f32[2,128,512]{2,1,0:T(8,128)S(1)} %get-tuple-element.63), channel_id=1, source_target_pairs={{0,4},{4,0},{8,12},{12,8},{16,20},{20,16},{24,28},{28,24},{1,5},{5... | collective-permute-start | bytes 1572872 | tf_op jit(solution)/shard_map/ppermute | solution.py:570
  23.4 7.6 %collective-permute-start.6 = (f32[2,128,512]{2,1,0:T(8,128)S(1)}, f32[2,128,512]{2,1,0:T(8,128)S(1)}, u32[]{:S(2)}, u32[]{:S(2)}) collective-permute-start(f32[2,128,512]{2,1,0:T(8,128)S(1)} %get-tuple-element.68), channel_id=1, source_target_pairs={{4,8},{8,4},{12,16},{16,12},{20,24},{24,20},{5,9},{9,5},{13,17},{1... | collective-permute-start | bytes 1572872 | tf_op jit(solution)/shard_map/ppermute | solution.py:575
  24.1 6.9 %collective-permute-start.7 = (f32[2,128,512]{2,1,0:T(8,128)S(1)}, f32[2,128,512]{2,1,0:T(8,128)S(1)}, u32[]{:S(2)}, u32[]{:S(2)}) collective-permute-start(f32[2,128,512]{2,1,0:T(8,128)S(1)} %get-tuple-element.69), channel_id=1, source_target_pairs={{0,4},{4,0},{8,12},{12,8},{16,20},{20,16},{24,28},{28,24},{1,5},{5... | collective-permute-start | bytes 1572872 | tf_op jit(solution)/shard_map/ppermute | solution.py:570
  35.6 11.4 %collective-permute-start.9 = (f32[2,128,512]{2,1,0:T(8,128)S(1)}, f32[2,128,512]{2,1,0:T(8,128)S(1)}, u32[]{:S(2)}, u32[]{:S(2)}) collective-permute-start(f32[2,128,512]{2,1,0:T(8,128)S(1)} %get-tuple-element.84), channel_id=1, source_target_pairs={{4,8},{8,4},{12,16},{16,12},{20,24},{24,20},{5,9},{9,5},{13,17},{1... | collective-permute-start | bytes 1572872 | tf_op jit(solution)/shard_map/ppermute | solution.py:575
  36.3 10.8 %collective-permute-start.10 = (f32[2,128,512]{2,1,0:T(8,128)S(1)}, f32[2,128,512]{2,1,0:T(8,128)S(1)}, u32[]{:S(2)}, u32[]{:S(2)}) collective-permute-start(f32[2,128,512]{2,1,0:T(8,128)S(1)} %get-tuple-element.85), channel_id=1, source_target_pairs={{0,4},{4,0},{8,12},{12,8},{16,20},{20,16},{24,28},{28,24},{1,5},{5... | collective-permute-start | bytes 1572872 | tf_op jit(solution)/shard_map/ppermute | solution.py:570
  47.0 17.0 %collective-permute-start.11 = (f32[136,256]{1,0:T(8,128)S(1)}, f32[136,256]{1,0:T(8,128)S(1)}, u32[]{:S(2)}, u32[]{:S(2)}) collective-permute-start(f32[136,256]{1,0:T(8,128)S(1)} %get-tuple-element.86), channel_id=1, source_target_pairs={{0,8},{4,12},{8,0},{12,4},{16,24},{20,28},{24,16},{28,20},{1,9},{5... | collective-permute-start | bytes 417800 | tf_op jit(solution)/shard_map/ppermute | solution.py:570
  51.5 25.9 %collective-permute-start.15 = (f32[2,256,128]{2,1,0:T(8,128)S(1)}, f32[2,256,128]{2,1,0:T(8,128)S(1)}, u32[]{:S(2)}, u32[]{:S(2)}) collective-permute-start(f32[2,256,128]{2,1,0:T(8,128)S(1)} %get-tuple-element.94), channel_id=1, source_target_pairs={{0,1},{1,0},{2,3},{3,2},{4,5},{5,4},{6,7},{7,6},{8,9},{9,8},{10,11... | collective-permute-start | bytes 786440 | tf_op jit(solution)/shard_map/ppermute | solution.py:570
  59.7 17.7 %collective-permute-start.16 = (f32[2,256,128]{2,1,0:T(8,128)S(1)}, f32[2,256,128]{2,1,0:T(8,128)S(1)}, u32[]{:S(2)}, u32[]{:S(2)}) collective-permute-start(f32[2,256,128]{2,1,0:T(8,128)S(1)} %get-tuple-element.95), channel_id=1, source_target_pairs={{1,2},{2,1},{5,6},{6,5},{9,10},{10,9},{13,14},{14,13},{17,18},{18,... | collective-permute-start | bytes 786440 | tf_op jit(solution)/shard_map/ppermute | solution.py:575
  60.4 17.0 %collective-permute-start.13 = (f32[2,128,512]{2,1,0:T(8,128)S(1)}, f32[2,128,512]{2,1,0:T(8,128)S(1)}, u32[]{:S(2)}, u32[]{:S(2)}) collective-permute-start(f32[2,128,512]{2,1,0:T(8,128)S(1)} %get-tuple-element.89), channel_id=1, source_target_pairs={{4,8},{8,4},{12,16},{16,12},{20,24},{24,20},{5,9},{9,5},{13,17},{1... | collective-permute-start | bytes 1572872 | tf_op jit(solution)/shard_map/ppermute | solution.py:575
  61.1 16.3 %collective-permute-start.14 = (f32[2,128,512]{2,1,0:T(8,128)S(1)}, f32[2,128,512]{2,1,0:T(8,128)S(1)}, u32[]{:S(2)}, u32[]{:S(2)}) collective-permute-start(f32[2,128,512]{2,1,0:T(8,128)S(1)} %get-tuple-element.90), channel_id=1, source_target_pairs={{0,4},{4,0},{8,12},{12,8},{16,20},{20,16},{24,28},{28,24},{1,5},{5... | collective-permute-start | bytes 1572872 | tf_op jit(solution)/shard_map/ppermute | solution.py:570
  64.1 13.3 %collective-permute-start.12 = (f32[72,256]{1,0:T(8,128)S(1)}, f32[72,256]{1,0:T(8,128)S(1)}, u32[]{:S(2)}, u32[]{:S(2)}) collective-permute-start(f32[72,256]{1,0:T(8,128)S(1)} %get-tuple-element.88), channel_id=1, source_target_pairs={{0,16},{4,20},{8,24},{12,28},{16,0},{20,4},{24,8},{28,12},{1,17},{... | collective-permute-start | bytes 221192 | tf_op jit(solution)/shard_map/ppermute | solution.py:570
  77.4 6.2 %collective-permute-start.19 = (f32[72,256]{1,0:T(8,128)S(1)}, f32[72,256]{1,0:T(8,128)S(1)}, u32[]{:S(2)}, u32[]{:S(2)}) collective-permute-start(f32[72,256]{1,0:T(8,128)S(1)} %add.6.refs_0_), channel_id=1, source_target_pairs={{0,3},{1,2},{2,1},{3,0},{4,7},{5,6},{6,5},{7,4},{8,11},{9,10},{10,... | collective-permute-start | bytes 221192 | tf_op jit(solution)/shard_map/ppermute | solution.py:570
  78.0 6.9 %collective-permute-start.18 = (f32[72,256]{1,0:T(8,128)S(1)}, f32[72,256]{1,0:T(8,128)S(1)}, u32[]{:S(2)}, u32[]{:S(2)}) collective-permute-start(f32[72,256]{1,0:T(8,128)S(1)} %add.6.refs_0_), channel_id=1, source_target_pairs={{0,2},{1,3},{2,0},{3,1},{4,6},{5,7},{6,4},{7,5},{8,10},{9,11},{10,... | collective-permute-start | bytes 221192 | tf_op jit(solution)/shard_map/ppermute | solution.py:570
  80.7 5.7 %collective-permute-start.17 = (f32[72,256]{1,0:T(8,128)S(1)}, f32[72,256]{1,0:T(8,128)S(1)}, u32[]{:S(2)}, u32[]{:S(2)}) collective-permute-start(f32[72,256]{1,0:T(8,128)S(1)} %add.6.refs_0_), channel_id=1, source_target_pairs={{0,1},{1,0},{2,3},{3,2},{4,5},{5,4},{6,7},{7,6},{8,9},{9,8},{10,11... | collective-permute-start | bytes 221192 | tf_op jit(solution)/shard_map/ppermute | solution.py:570
  81.9 12.2 %collective-permute-start.24 = (f32[2,256,128]{2,1,0:T(8,128)S(1)}, f32[2,256,128]{2,1,0:T(8,128)S(1)}, u32[]{:S(2)}, u32[]{:S(2)}) collective-permute-start(f32[2,256,128]{2,1,0:T(8,128)S(1)} %get-tuple-element.101), channel_id=1, source_target_pairs={{0,1},{1,0},{2,3},{3,2},{4,5},{5,4},{6,7},{7,6},{8,9},{9,8},{10,11... | collective-permute-start | bytes 786440 | tf_op jit(solution)/shard_map/ppermute | solution.py:570
  83.0 11.1 %collective-permute-start.25 = (f32[2,256,128]{2,1,0:T(8,128)S(1)}, f32[2,256,128]{2,1,0:T(8,128)S(1)}, u32[]{:S(2)}, u32[]{:S(2)}) collective-permute-start(f32[2,256,128]{2,1,0:T(8,128)S(1)} %get-tuple-element.102), channel_id=1, source_target_pairs={{1,2},{2,1},{5,6},{6,5},{9,10},{10,9},{13,14},{14,13},{17,18},{18,... | collective-permute-start | bytes 786440 | tf_op jit(solution)/shard_map/ppermute | solution.py:575
  86.4 6.7 %collective-permute-start.22 = (f32[64,256]{1,0:T(8,128)S(1)}, f32[64,256]{1,0:T(8,128)S(1)}, u32[]{:S(2)}, u32[]{:S(2)}) collective-permute-start(f32[64,256]{1,0:T(8,128)S(1)} %slice.8.refs_0_), channel_id=1, source_target_pairs={{0,24},{4,28},{8,16},{12,20},{16,8},{20,12},{24,0},{28,4},{1,25},{... | collective-permute-start | bytes 196616 | tf_op jit(solution)/shard_map/ppermute | solution.py:570
  86.5 6.6 %collective-permute-start.21 = (f32[64,256]{1,0:T(8,128)S(1)}, f32[64,256]{1,0:T(8,128)S(1)}, u32[]{:S(2)}, u32[]{:S(2)}) collective-permute-start(f32[64,256]{1,0:T(8,128)S(1)} %slice.8.refs_0_), channel_id=1, source_target_pairs={{0,8},{4,12},{8,0},{12,4},{16,24},{20,28},{24,16},{28,20},{1,9},{5... | collective-permute-start | bytes 196616 | tf_op jit(solution)/shard_map/ppermute | solution.py:570
  87.6 6.4 %collective-permute-start.20 = (f32[64,256]{1,0:T(8,128)S(1)}, f32[64,256]{1,0:T(8,128)S(1)}, u32[]{:S(2)}, u32[]{:S(2)}) collective-permute-start(f32[64,256]{1,0:T(8,128)S(1)} %slice.8.refs_0_), channel_id=1, source_target_pairs={{0,16},{4,20},{8,24},{12,28},{16,0},{20,4},{24,8},{28,12},{1,17},{... | collective-permute-start | bytes 196616 | tf_op jit(solution)/shard_map/ppermute | solution.py:570
  (10 other events, 37.9 us)

commit v4 on v3

--- a/solution.py
+++ b/solution.py
@@ -49,20 +49,20 @@
 
 def right_dot(value, matrix):
     high, low = split(value)
-    return jnp.dot(
-        jnp.concatenate([high, low, high], axis=1),
-        jnp.concatenate([matrix[0], matrix[0], matrix[1]], axis=0),
-        preferred_element_type=F32,
-    )
+    rows = value.shape[0]
+    both = jnp.dot(jnp.concatenate([high, low], axis=0), matrix[0], preferred_element_type=F32)
+    rest = jnp.dot(high, matrix[1], preferred_element_type=F32)
+    return both[:rows] + (both[rows:] + rest)
 
 
 def left_dot(matrix, value):
     high, low = split(value)
-    return jnp.dot(
-        jnp.concatenate([matrix[0], matrix[0], matrix[1]], axis=1),
-        jnp.concatenate([high, low, high], axis=0),
-        preferred_element_type=F32,
-    )
+    rows = matrix[0].shape[0]
+    both = jnp.dot(
+        jnp.concatenate([matrix[0], matrix[1]], axis=0), high, preferred_element_type=F32
+    )
+    rest = jnp.dot(matrix[0], low, preferred_element_type=F32)
+    return both[:rows] + (both[rows:] + rest)
 
 
 def mul(a, b):

time: 96.9 us -> 95.5 us (0.986)
  starting transfers between devices: 54.1 us -> 45.4 us
  Pallas kernels: 17 us -> 25.5 us
    ppermute x18, starting transfers between devices: 48.6 us -> 39.9 us  [swap(): lax.ppermute(value, axis, [(i, i ^ bit) for i in range(lax.axis_size(axis...]
    pallas_call x16, Pallas kernels: 17 us -> 25.5 us  [call(): pl.pallas_call(kernel, out_shape=[jax.ShapeDtypeStruct(shape, F32) for sh...]
  transfers between devices with their start and end apart: 26 -> 26, of which waited for: 8 -> 7; matrix products, arithmetic and copies ran while one was open for 1% -> 1% of each run, Pallas kernels for 12% -> 18%
where the time goes in v4:
time: 95.5 us; the launch traced here: 95.4 us
  starting transfers between devices  45.4 us (48%)
  Pallas kernels  25.5 us (27%)
  waiting for transfers between devices  17.5 us (18%)
  local copies, waits for them, and re-layouts  5.34 us (6%)
  between operations  1.64 us (2%)
    ppermute x18, starting transfers between devices, swap(): lax.ppermute(value, axis, [(i, i ^ bit) for i in range(lax.axis_size(axis...  39.9 us
    pallas_call x16, Pallas kernels, call(): pl.pallas_call(kernel, out_shape=[jax.ShapeDtypeStruct(shape, F32) for sh...  25.5 us
    ppermute x18, waiting for transfers between devices, swap(): lax.ppermute(value, axis, [(i, i ^ bit) for i in range(lax.axis_size(axis...  17.5 us
    ppermute x8, starting transfers between devices, swap_next(): lax.ppermute(value, axis, [pair for i in odd for pair in ((i, i + 1), (i...  5.44 us
    unnamed x16, local copies, waits for them, and re-layouts  4.64 us
  transfers between devices with their start and end apart: 26, of which 7 were waited for; matrix products, arithmetic and copies ran while one was open for 1% of the time, Pallas kernels for 18%

profile of v4, /device:TPU:0, one launch (start us, length us, event | category | flops | bytes accessed | tf_op | source)
XLA Modules:
  0.0 95.4 jit_solution(13917197068643062127)
XLA Ops:
  0.6 1.2 %copy-done = f32[2,2,256,256]{3,2,1,0:T(8,128)S(1)} copy-done((f32[2,2,256,256]{3,2,1,0:T(8,128)S(1)}, f32[2,2,256,256]{3,2,1,0:T(8,128)}, u32[]{:S(2)}) %copy-start) | copy-done | bytes 1048600
  1.9 3.0 %collective-permute-start = (f32[2,256,128]{2,1,0:T(8,128)S(1)}, f32[2,256,128]{2,1,0:T(8,128)S(1)}, u32[]{:S(2)}, u32[]{:S(2)}) collective-permute-start(f32[2,256,128]{2,1,0:T(8,128)S(1)} %get-tuple-element.56), channel_id=1, source_target_pairs={{0,1},{1,0},{2,3},{3,2},{4,5},{5,4},{6,7},{7,6},{8,9},{9,8},{10,11... | collective-permute-start | bytes 786440 | tf_op jit(solution)/shard_map/ppermute | solution.py:570
  5.6 4.3 %collective-permute-start.4 = (f32[2,256,128]{2,1,0:T(8,128)S(1)}, f32[2,256,128]{2,1,0:T(8,128)S(1)}, u32[]{:S(2)}, u32[]{:S(2)}) collective-permute-start(f32[2,256,128]{2,1,0:T(8,128)S(1)} %get-tuple-element.66), channel_id=1, source_target_pairs={{0,1},{1,0},{2,3},{3,2},{4,5},{5,4},{6,7},{7,6},{8,9},{9,8},{10,11... | collective-permute-start | bytes 786440 | tf_op jit(solution)/shard_map/ppermute | solution.py:570
  11.9 1.2 %copy-done.3 = f32[1,1,4,256,256]{4,3,2,1,0:T(8,128)S(1)} copy-done((f32[1,1,4,256,256]{4,3,2,1,0:T(8,128)S(1)}, f32[1,1,4,256,256]{4,3,2,1,0:T(8,128)}, u32[]{:S(2)}) %copy-start.3) | copy-done | bytes 1048600
  14.2 1.1 %copy-done.5 = bf16[6,256,256]{2,1,0:T(8,128)(2,1)S(1)} copy-done((bf16[6,256,256]{2,1,0:T(8,128)(2,1)S(1)}, bf16[6,256,256]{2,1,0:T(8,128)(2,1)}, u32[]{:S(2)}) %copy-start.5) | copy-done | bytes 786456
  15.3 2.3 %reorder_targets.1 = (f32[4,256,256]{2,1,0:T(8,128)S(1)}, f32[2,256,256]{2,1,0:T(8,128)S(1)}, f32[8,256]{1,0:T(8,128)S(1)}) custom-call(s32[3,4]{1,0:T(4,128)S(1)} %concatenate.3.places, f32[4,256,256]{2,1,0:T(8,128)S(1)} %bitcast.6, f32[2,256,256]{2,1,0:T(8,128)S(1)} %copy-done.4, bf16[6,256,256]{2,1,0:T(8,128)(2,1)S(1)} %copy-done.5), custom_call_target="tpu_custom_call" | custom-call | flops 6000000000 | bytes 3145728 | tf_op jit(solution)/shard_map/reorder_targets/pallas_call | solution.py:557
  18.4 3.0 %collective-permute-start.3 = (f32[2,128,512]{2,1,0:T(8,128)S(1)}, f32[2,128,512]{2,1,0:T(8,128)S(1)}, u32[]{:S(2)}, u32[]{:S(2)}) collective-permute-start(f32[2,128,512]{2,1,0:T(8,128)S(1)} %get-tuple-element.63), channel_id=1, source_target_pairs={{0,4},{4,0},{8,12},{12,8},{16,20},{20,16},{24,28},{28,24},{1,5},{5... | collective-permute-start | bytes 1572872 | tf_op jit(solution)/shard_map/ppermute | solution.py:570
  21.4 1.9 %collective-permute-done.4.side_a = f32[2,256,128]{2,1,0:T(8,128)S(1)} collective-permute-done((f32[2,256,128]{2,1,0:T(8,128)S(1)}, f32[2,256,128]{2,1,0:T(8,128)S(1)}, u32[]{:S(2)}, u32[]{:S(2)}) %collective-permute-start.4) | collective-permute-done | bytes 262176 | tf_op jit(solution)/shard_map/ppermute | solution.py:570
  24.1 3.5 %collective-permute-start.7 = (f32[2,128,512]{2,1,0:T(8,128)S(1)}, f32[2,128,512]{2,1,0:T(8,128)S(1)}, u32[]{:S(2)}, u32[]{:S(2)}) collective-permute-start(f32[2,128,512]{2,1,0:T(8,128)S(1)} %get-tuple-element.69), channel_id=1, source_target_pairs={{0,4},{4,0},{8,12},{12,8},{16,20},{20,16},{24,28},{28,24},{1,5},{5... | collective-permute-start | bytes 1572872 | tf_op jit(solution)/shard_map/ppermute | solution.py:570
  27.7 5.9 %first_slice.1 = (f32[4,2,256,256]{3,2,1,0:T(8,128)S(1)}, f32[4,2,256,256]{3,2,1,0:T(8,128)S(1)}) custom-call(s32[3,4]{1,0:T(4,128)S(1)} %concatenate.3.places, f32[2,2,256,256]{3,2,1,0:T(8,128)S(1)} %copy-done.1, f32[2,256,128]{2,1,0:T(8,128)S(1)} %collective-permute-done.side_a, f32[2,256,128]{2,1,0:T(8,128)S(1)} %collective-permute-done.1.side_b, ...), custom_call_target="tpu_custom_call" | custom-call | flops 20000000000 | bytes 5382144 | tf_op jit(solution)/shard_map/first_slice/pallas_call | solution.py:557
  33.7 7.8 %second_slice.1 = (f32[4,2,256,256]{3,2,1,0:T(8,128)S(1)}, f32[2,256,512]{2,1,0:T(8,128)S(1)}, f32[2,128,512]{2,1,0:T(8,128)S(1)}, f32[2,128,512]{2,1,0:T(8,128)S(1)}) custom-call(s32[3,4]{1,0:T(4,128)S(1)} %concatenate.3.places, f32[2,2,256,256]{3,2,1,0:T(8,128)S(1)} %copy-done.1, f32[2,256,128]{2,1,0:T(8,128)S(1)} %collective-permute-done.4.side_a, ...), custom_call_target="tpu_custom_call" | custom-call | flops 20000000000 | bytes 7479296 | tf_op jit(solution)/shard_map/second_slice/pallas_call | solution.py:557
  42.6 4.7 %first_adjoint.1 = (f32[4,2,256,256]{3,2,1,0:T(8,128)S(1)}, f32[264,256]{1,0:T(8,128)S(1)}, f32[264,256]{1,0:T(8,128)S(1)}) custom-call(s32[3,4]{1,0:T(4,128)S(1)} %concatenate.3.places, f32[8,256]{1,0:T(8,128)S(1)} %get-tuple-element.55.level_scalars, f32[4,2,256,256]{3,2,1,0:T(8,128)S(1)} %get-tuple-element.65.patches, ...), custom_call_target="tpu_custom_call" | custom-call | flops 20000000000 | bytes 6963200 | tf_op jit(solution)/shard_map/first_adjoint/pallas_call | solution.py:557
  47.4 2.1 %first_gradient.1 = (f32[2,256,512]{2,1,0:T(8,128)S(1)}, f32[2,128,512]{2,1,0:T(8,128)S(1)}, f32[2,128,512]{2,1,0:T(8,128)S(1)}) custom-call(s32[3,4]{1,0:T(4,128)S(1)} %concatenate.3.places, f32[2,256,256]{2,1,0:T(8,128)S(1)} %copy-done.2, f32[4,2,256,256]{3,2,1,0:T(8,128)S(1)} %get-tuple-element.75.adjoints), custom_call_target="tpu_custom_call" | custom-call | bytes 2621440 | tf_op jit(solution)/shard_map/first_gradient/pallas_call | solution.py:557
  49.6 2.6 %collective-permute-start.11 = (f32[136,256]{1,0:T(8,128)S(1)}, f32[136,256]{1,0:T(8,128)S(1)}, u32[]{:S(2)}, u32[]{:S(2)}) collective-permute-start(f32[136,256]{1,0:T(8,128)S(1)} %get-tuple-element.86), channel_id=1, source_target_pairs={{0,8},{4,12},{8,0},{12,4},{16,24},{20,28},{24,16},{28,20},{1,9},{5... | collective-permute-start | bytes 417800 | tf_op jit(solution)/shard_map/ppermute | solution.py:570
  52.4 7.4 %collective-permute-start.15 = (f32[2,256,128]{2,1,0:T(8,128)S(1)}, f32[2,256,128]{2,1,0:T(8,128)S(1)}, u32[]{:S(2)}, u32[]{:S(2)}) collective-permute-start(f32[2,256,128]{2,1,0:T(8,128)S(1)} %get-tuple-element.94), channel_id=1, source_target_pairs={{0,1},{1,0},{2,3},{3,2},{4,5},{5,4},{6,7},{7,6},{8,9},{9,8},{10,11... | collective-permute-start | bytes 786440 | tf_op jit(solution)/shard_map/ppermute | solution.py:570
  61.2 1.5 %collective-permute-start.14 = (f32[2,128,512]{2,1,0:T(8,128)S(1)}, f32[2,128,512]{2,1,0:T(8,128)S(1)}, u32[]{:S(2)}, u32[]{:S(2)}) collective-permute-start(f32[2,128,512]{2,1,0:T(8,128)S(1)} %get-tuple-element.90), channel_id=1, source_target_pairs={{0,4},{4,0},{8,12},{12,8},{16,20},{20,16},{24,28},{28,24},{1,5},{5... | collective-permute-start | bytes 1572872 | tf_op jit(solution)/shard_map/ppermute | solution.py:570
  62.7 2.5 %collective-permute-start.12 = (f32[72,256]{1,0:T(8,128)S(1)}, f32[72,256]{1,0:T(8,128)S(1)}, u32[]{:S(2)}, u32[]{:S(2)}) collective-permute-start(f32[72,256]{1,0:T(8,128)S(1)} %get-tuple-element.88), channel_id=1, source_target_pairs={{0,16},{4,20},{8,24},{12,28},{16,0},{20,4},{24,8},{28,12},{1,17},{... | collective-permute-start | bytes 221192 | tf_op jit(solution)/shard_map/ppermute | solution.py:570
  65.2 10.1 %collective-permute-done.12 = f32[72,256]{1,0:T(8,128)S(1)} collective-permute-done((f32[72,256]{1,0:T(8,128)S(1)}, f32[72,256]{1,0:T(8,128)S(1)}, u32[]{:S(2)}, u32[]{:S(2)}) %collective-permute-start.12) | collective-permute-done | bytes 73760 | tf_op jit(solution)/shard_map/ppermute | solution.py:570
  75.4 2.3 %collective-permute-start.19 = (f32[72,256]{1,0:T(8,128)S(1)}, f32[72,256]{1,0:T(8,128)S(1)}, u32[]{:S(2)}, u32[]{:S(2)}) collective-permute-start(f32[72,256]{1,0:T(8,128)S(1)} %add.6.refs_0_), channel_id=1, source_target_pairs={{0,3},{1,2},{2,1},{3,0},{4,7},{5,6},{6,5},{7,4},{8,11},{9,10},{10,... | collective-permute-start | bytes 221192 | tf_op jit(solution)/shard_map/ppermute | solution.py:570
  77.6 2.7 %collective-permute-start.18 = (f32[72,256]{1,0:T(8,128)S(1)}, f32[72,256]{1,0:T(8,128)S(1)}, u32[]{:S(2)}, u32[]{:S(2)}) collective-permute-start(f32[72,256]{1,0:T(8,128)S(1)} %add.6.refs_0_), channel_id=1, source_target_pairs={{0,2},{1,3},{2,0},{3,1},{4,6},{5,7},{6,4},{7,5},{8,10},{9,11},{10,... | collective-permute-start | bytes 221192 | tf_op jit(solution)/shard_map/ppermute | solution.py:570
  80.6 2.1 %collective-permute-start.24 = (f32[2,256,128]{2,1,0:T(8,128)S(1)}, f32[2,256,128]{2,1,0:T(8,128)S(1)}, u32[]{:S(2)}, u32[]{:S(2)}) collective-permute-start(f32[2,256,128]{2,1,0:T(8,128)S(1)} %get-tuple-element.101), channel_id=1, source_target_pairs={{0,1},{1,0},{2,3},{3,2},{4,5},{5,4},{6,7},{7,6},{8,9},{9,8},{10,11... | collective-permute-start | bytes 786440 | tf_op jit(solution)/shard_map/ppermute | solution.py:570
  84.4 1.1 %collective-permute-done.17.refs_1_ = f32[72,256]{1,0:T(8,128)S(1)} collective-permute-done((f32[72,256]{1,0:T(8,128)S(1)}, f32[72,256]{1,0:T(8,128)S(1)}, u32[]{:S(2)}, u32[]{:S(2)}) %collective-permute-start.17) | collective-permute-done | bytes 73760 | tf_op jit(solution)/shard_map/ppermute | solution.py:570
  86.8 3.3 %collective-permute-start.20 = (f32[64,256]{1,0:T(8,128)S(1)}, f32[64,256]{1,0:T(8,128)S(1)}, u32[]{:S(2)}, u32[]{:S(2)}) collective-permute-start(f32[64,256]{1,0:T(8,128)S(1)} %slice.8.refs_0_), channel_id=1, source_target_pairs={{0,16},{4,20},{8,24},{12,28},{16,0},{20,4},{24,8},{28,12},{1,17},{... | collective-permute-start | bytes 196616 | tf_op jit(solution)/shard_map/ppermute | solution.py:570
  90.0 2.3 %collective-permute-done.22.refs_3_ = f32[64,256]{1,0:T(8,128)S(1)} collective-permute-done((f32[64,256]{1,0:T(8,128)S(1)}, f32[64,256]{1,0:T(8,128)S(1)}, u32[]{:S(2)}, u32[]{:S(2)}) %collective-permute-start.22) | collective-permute-done | bytes 65568 | tf_op jit(solution)/shard_map/ppermute | solution.py:570
  (64 shorter events, 13.8 us)
Async XLA Ops:
  1.9 15.6 %collective-permute-start = (f32[2,256,128]{2,1,0:T(8,128)S(1)}, f32[2,256,128]{2,1,0:T(8,128)S(1)}, u32[]{:S(2)}, u32[]{:S(2)}) collective-permute-start(f32[2,256,128]{2,1,0:T(8,128)S(1)} %get-tuple-element.56), channel_id=1, source_target_pairs={{0,1},{1,0},{2,3},{3,2},{4,5},{5,4},{6,7},{7,6},{8,9},{9,8},{10,11... | collective-permute-start | bytes 786440 | tf_op jit(solution)/shard_map/ppermute | solution.py:570
  4.9 12.6 %collective-permute-start.1 = (f32[2,256,128]{2,1,0:T(8,128)S(1)}, f32[2,256,128]{2,1,0:T(8,128)S(1)}, u32[]{:S(2)}, u32[]{:S(2)}) collective-permute-start(f32[2,256,128]{2,1,0:T(8,128)S(1)} %get-tuple-element.57), channel_id=1, source_target_pairs={{1,2},{2,1},{5,6},{6,5},{9,10},{10,9},{13,14},{14,13},{17,18},{18,... | collective-permute-start | bytes 786440 | tf_op jit(solution)/shard_map/ppermute | solution.py:575
  5.6 17.7 %collective-permute-start.4 = (f32[2,256,128]{2,1,0:T(8,128)S(1)}, f32[2,256,128]{2,1,0:T(8,128)S(1)}, u32[]{:S(2)}, u32[]{:S(2)}) collective-permute-start(f32[2,256,128]{2,1,0:T(8,128)S(1)} %get-tuple-element.66), channel_id=1, source_target_pairs={{0,1},{1,0},{2,3},{3,2},{4,5},{5,4},{6,7},{7,6},{8,9},{9,8},{10,11... | collective-permute-start | bytes 786440 | tf_op jit(solution)/shard_map/ppermute | solution.py:570
  9.9 13.4 %collective-permute-start.5 = (f32[2,256,128]{2,1,0:T(8,128)S(1)}, f32[2,256,128]{2,1,0:T(8,128)S(1)}, u32[]{:S(2)}, u32[]{:S(2)}) collective-permute-start(f32[2,256,128]{2,1,0:T(8,128)S(1)} %get-tuple-element.67), channel_id=1, source_target_pairs={{1,2},{2,1},{5,6},{6,5},{9,10},{10,9},{13,14},{14,13},{17,18},{18,... | collective-permute-start | bytes 786440 | tf_op jit(solution)/shard_map/ppermute | solution.py:575
  17.7 10.0 %collective-permute-start.2 = (f32[2,128,512]{2,1,0:T(8,128)S(1)}, f32[2,128,512]{2,1,0:T(8,128)S(1)}, u32[]{:S(2)}, u32[]{:S(2)}) collective-permute-start(f32[2,128,512]{2,1,0:T(8,128)S(1)} %get-tuple-element.62), channel_id=1, source_target_pairs={{4,8},{8,4},{12,16},{16,12},{20,24},{24,20},{5,9},{9,5},{13,17},{1... | collective-permute-start | bytes 1572872 | tf_op jit(solution)/shard_map/ppermute | solution.py:575
  18.4 9.2 %collective-permute-start.3 = (f32[2,128,512]{2,1,0:T(8,128)S(1)}, f32[2,128,512]{2,1,0:T(8,128)S(1)}, u32[]{:S(2)}, u32[]{:S(2)}) collective-permute-start(f32[2,128,512]{2,1,0:T(8,128)S(1)} %get-tuple-element.63), channel_id=1, source_target_pairs={{0,4},{4,0},{8,12},{12,8},{16,20},{20,16},{24,28},{28,24},{1,5},{5... | collective-permute-start | bytes 1572872 | tf_op jit(solution)/shard_map/ppermute | solution.py:570
  23.4 10.2 %collective-permute-start.6 = (f32[2,128,512]{2,1,0:T(8,128)S(1)}, f32[2,128,512]{2,1,0:T(8,128)S(1)}, u32[]{:S(2)}, u32[]{:S(2)}) collective-permute-start(f32[2,128,512]{2,1,0:T(8,128)S(1)} %get-tuple-element.68), channel_id=1, source_target_pairs={{4,8},{8,4},{12,16},{16,12},{20,24},{24,20},{5,9},{9,5},{13,17},{1... | collective-permute-start | bytes 1572872 | tf_op jit(solution)/shard_map/ppermute | solution.py:575
  24.1 9.5 %collective-permute-start.7 = (f32[2,128,512]{2,1,0:T(8,128)S(1)}, f32[2,128,512]{2,1,0:T(8,128)S(1)}, u32[]{:S(2)}, u32[]{:S(2)}) collective-permute-start(f32[2,128,512]{2,1,0:T(8,128)S(1)} %get-tuple-element.69), channel_id=1, source_target_pairs={{0,4},{4,0},{8,12},{12,8},{16,20},{20,16},{24,28},{28,24},{1,5},{5... | collective-permute-start | bytes 1572872 | tf_op jit(solution)/shard_map/ppermute | solution.py:570
  41.5 8.1 %collective-permute-start.9 = (f32[2,128,512]{2,1,0:T(8,128)S(1)}, f32[2,128,512]{2,1,0:T(8,128)S(1)}, u32[]{:S(2)}, u32[]{:S(2)}) collective-permute-start(f32[2,128,512]{2,1,0:T(8,128)S(1)} %get-tuple-element.84), channel_id=1, source_target_pairs={{4,8},{8,4},{12,16},{16,12},{20,24},{24,20},{5,9},{9,5},{13,17},{1... | collective-permute-start | bytes 1572872 | tf_op jit(solution)/shard_map/ppermute | solution.py:575
  42.2 7.4 %collective-permute-start.10 = (f32[2,128,512]{2,1,0:T(8,128)S(1)}, f32[2,128,512]{2,1,0:T(8,128)S(1)}, u32[]{:S(2)}, u32[]{:S(2)}) collective-permute-start(f32[2,128,512]{2,1,0:T(8,128)S(1)} %get-tuple-element.85), channel_id=1, source_target_pairs={{0,4},{4,0},{8,12},{12,8},{16,20},{20,16},{24,28},{28,24},{1,5},{5... | collective-permute-start | bytes 1572872 | tf_op jit(solution)/shard_map/ppermute | solution.py:570
  49.6 13.1 %collective-permute-start.11 = (f32[136,256]{1,0:T(8,128)S(1)}, f32[136,256]{1,0:T(8,128)S(1)}, u32[]{:S(2)}, u32[]{:S(2)}) collective-permute-start(f32[136,256]{1,0:T(8,128)S(1)} %get-tuple-element.86), channel_id=1, source_target_pairs={{0,8},{4,12},{8,0},{12,4},{16,24},{20,28},{24,16},{28,20},{1,9},{5... | collective-permute-start | bytes 417800 | tf_op jit(solution)/shard_map/ppermute | solution.py:570
  52.4 22.9 %collective-permute-start.15 = (f32[2,256,128]{2,1,0:T(8,128)S(1)}, f32[2,256,128]{2,1,0:T(8,128)S(1)}, u32[]{:S(2)}, u32[]{:S(2)}) collective-permute-start(f32[2,256,128]{2,1,0:T(8,128)S(1)} %get-tuple-element.94), channel_id=1, source_target_pairs={{0,1},{1,0},{2,3},{3,2},{4,5},{5,4},{6,7},{7,6},{8,9},{9,8},{10,11... | collective-permute-start | bytes 786440 | tf_op jit(solution)/shard_map/ppermute | solution.py:570
  59.8 15.5 %collective-permute-start.16 = (f32[2,256,128]{2,1,0:T(8,128)S(1)}, f32[2,256,128]{2,1,0:T(8,128)S(1)}, u32[]{:S(2)}, u32[]{:S(2)}) collective-permute-start(f32[2,256,128]{2,1,0:T(8,128)S(1)} %get-tuple-element.95), channel_id=1, source_target_pairs={{1,2},{2,1},{5,6},{6,5},{9,10},{10,9},{13,14},{14,13},{17,18},{18,... | collective-permute-start | bytes 786440 | tf_op jit(solution)/shard_map/ppermute | solution.py:575
  60.5 14.9 %collective-permute-start.13 = (f32[2,128,512]{2,1,0:T(8,128)S(1)}, f32[2,128,512]{2,1,0:T(8,128)S(1)}, u32[]{:S(2)}, u32[]{:S(2)}) collective-permute-start(f32[2,128,512]{2,1,0:T(8,128)S(1)} %get-tuple-element.89), channel_id=1, source_target_pairs={{4,8},{8,4},{12,16},{16,12},{20,24},{24,20},{5,9},{9,5},{13,17},{1... | collective-permute-start | bytes 1572872 | tf_op jit(solution)/shard_map/ppermute | solution.py:575
  61.2 14.2 %collective-permute-start.14 = (f32[2,128,512]{2,1,0:T(8,128)S(1)}, f32[2,128,512]{2,1,0:T(8,128)S(1)}, u32[]{:S(2)}, u32[]{:S(2)}) collective-permute-start(f32[2,128,512]{2,1,0:T(8,128)S(1)} %get-tuple-element.90), channel_id=1, source_target_pairs={{0,4},{4,0},{8,12},{12,8},{16,20},{20,16},{24,28},{28,24},{1,5},{5... | collective-permute-start | bytes 1572872 | tf_op jit(solution)/shard_map/ppermute | solution.py:570
  62.7 12.6 %collective-permute-start.12 = (f32[72,256]{1,0:T(8,128)S(1)}, f32[72,256]{1,0:T(8,128)S(1)}, u32[]{:S(2)}, u32[]{:S(2)}) collective-permute-start(f32[72,256]{1,0:T(8,128)S(1)} %get-tuple-element.88), channel_id=1, source_target_pairs={{0,16},{4,20},{8,24},{12,28},{16,0},{20,4},{24,8},{28,12},{1,17},{... | collective-permute-start | bytes 221192 | tf_op jit(solution)/shard_map/ppermute | solution.py:570
  75.4 8.0 %collective-permute-start.19 = (f32[72,256]{1,0:T(8,128)S(1)}, f32[72,256]{1,0:T(8,128)S(1)}, u32[]{:S(2)}, u32[]{:S(2)}) collective-permute-start(f32[72,256]{1,0:T(8,128)S(1)} %add.6.refs_0_), channel_id=1, source_target_pairs={{0,3},{1,2},{2,1},{3,0},{4,7},{5,6},{6,5},{7,4},{8,11},{9,10},{10,... | collective-permute-start | bytes 221192 | tf_op jit(solution)/shard_map/ppermute | solution.py:570
  77.6 6.8 %collective-permute-start.18 = (f32[72,256]{1,0:T(8,128)S(1)}, f32[72,256]{1,0:T(8,128)S(1)}, u32[]{:S(2)}, u32[]{:S(2)}) collective-permute-start(f32[72,256]{1,0:T(8,128)S(1)} %add.6.refs_0_), channel_id=1, source_target_pairs={{0,2},{1,3},{2,0},{3,1},{4,6},{5,7},{6,4},{7,5},{8,10},{9,11},{10,... | collective-permute-start | bytes 221192 | tf_op jit(solution)/shard_map/ppermute | solution.py:570
  80.4 5.2 %collective-permute-start.17 = (f32[72,256]{1,0:T(8,128)S(1)}, f32[72,256]{1,0:T(8,128)S(1)}, u32[]{:S(2)}, u32[]{:S(2)}) collective-permute-start(f32[72,256]{1,0:T(8,128)S(1)} %add.6.refs_0_), channel_id=1, source_target_pairs={{0,1},{1,0},{2,3},{3,2},{4,5},{5,4},{6,7},{7,6},{8,9},{9,8},{10,11... | collective-permute-start | bytes 221192 | tf_op jit(solution)/shard_map/ppermute | solution.py:570
  80.6 12.5 %collective-permute-start.24 = (f32[2,256,128]{2,1,0:T(8,128)S(1)}, f32[2,256,128]{2,1,0:T(8,128)S(1)}, u32[]{:S(2)}, u32[]{:S(2)}) collective-permute-start(f32[2,256,128]{2,1,0:T(8,128)S(1)} %get-tuple-element.101), channel_id=1, source_target_pairs={{0,1},{1,0},{2,3},{3,2},{4,5},{5,4},{6,7},{7,6},{8,9},{9,8},{10,11... | collective-permute-start | bytes 786440 | tf_op jit(solution)/shard_map/ppermute | solution.py:570
  82.7 10.4 %collective-permute-start.25 = (f32[2,256,128]{2,1,0:T(8,128)S(1)}, f32[2,256,128]{2,1,0:T(8,128)S(1)}, u32[]{:S(2)}, u32[]{:S(2)}) collective-permute-start(f32[2,256,128]{2,1,0:T(8,128)S(1)} %get-tuple-element.102), channel_id=1, source_target_pairs={{1,2},{2,1},{5,6},{6,5},{9,10},{10,9},{13,14},{14,13},{17,18},{18,... | collective-permute-start | bytes 786440 | tf_op jit(solution)/shard_map/ppermute | solution.py:575
  85.6 6.7 %collective-permute-start.22 = (f32[64,256]{1,0:T(8,128)S(1)}, f32[64,256]{1,0:T(8,128)S(1)}, u32[]{:S(2)}, u32[]{:S(2)}) collective-permute-start(f32[64,256]{1,0:T(8,128)S(1)} %slice.8.refs_0_), channel_id=1, source_target_pairs={{0,24},{4,28},{8,16},{12,20},{16,8},{20,12},{24,0},{28,4},{1,25},{... | collective-permute-start | bytes 196616 | tf_op jit(solution)/shard_map/ppermute | solution.py:570
  85.7 6.6 %collective-permute-start.21 = (f32[64,256]{1,0:T(8,128)S(1)}, f32[64,256]{1,0:T(8,128)S(1)}, u32[]{:S(2)}, u32[]{:S(2)}) collective-permute-start(f32[64,256]{1,0:T(8,128)S(1)} %slice.8.refs_0_), channel_id=1, source_target_pairs={{0,8},{4,12},{8,0},{12,4},{16,24},{20,28},{24,16},{28,20},{1,9},{5... | collective-permute-start | bytes 196616 | tf_op jit(solution)/shard_map/ppermute | solution.py:570
  86.8 6.2 %collective-permute-start.20 = (f32[64,256]{1,0:T(8,128)S(1)}, f32[64,256]{1,0:T(8,128)S(1)}, u32[]{:S(2)}, u32[]{:S(2)}) collective-permute-start(f32[64,256]{1,0:T(8,128)S(1)} %slice.8.refs_0_), channel_id=1, source_target_pairs={{0,16},{4,20},{8,24},{12,28},{16,0},{20,4},{24,8},{28,12},{1,17},{... | collective-permute-start | bytes 196616 | tf_op jit(solution)/shard_map/ppermute | solution.py:570
  (10 other events, 38.4 us)
